TPU v7x, 32 devices: a whole 2x2x4 slice. The times are simulated.
32 devices in a mesh: seq: 8 (over z, y), tp: 4 (over x, core).
Axes of the slice: x: 2, y: 2, z: 4, core: 2. Of those that a mesh axis runs over, the one named last changes fastest.
Arguments:
- features: bfloat16 [2048, 3, 4096], P('seq', None, 'tp'), may hold values from -6 to 6
- short_taps: float32 [3, 7, 4096], P(None, None, 'tp'), may hold values from -2 to 2
- residue: float32 [16, 4096], P(None, 'tp'), may hold values from -1.5 to 1.5
- decay_rate: float32 [16, 4096], P(None, 'tp'), may hold values from 4.8828126e-05 to 0.05
- w_out: bfloat16 [4096, 4096], P('tp', 'seq'), may hold values from -0.09375 to 0.09375
- cotangent: bfloat16 [2048, 4096], P('seq', 'tp'), may hold values from -6 to 6
Outputs:
- mixed: bfloat16 [2048, 4096], P('seq', 'tp')
- grad_features: bfloat16 [2048, 3, 4096], P('seq', None, 'tp')
- grad_weight: float32 [4096, 4096], P('tp', 'seq')
- grad_taps: float32 [3, 7, 4096], P(None, None, 'tp')
- grad_residue: float32 [16, 4096], P(None, 'tp')
- grad_log_rate: float32 [16, 4096], P(None, 'tp')
All inputs are finite; a program needn't handle non-finite values.
Results may differ from a plain program's by a relative error of at most 0.013.
Values may be sent and summed in bfloat16 or wider, within the bound.
A program may use at most 128 MiB of HBM per device.

v0:
```python
import jax
import jax.numpy as jnp
from jax import lax
from jax.sharding import PartitionSpec as P


def shifted(array, axis, by):
    devices = lax.axis_size(axis)
    pairs = [(i, i + by) for i in range(devices) if 0 <= i + by < devices]
    return lax.ppermute(array, axis, pairs)


def pair_combine(earlier, later):
    return (earlier[0] * later[0], later[0] * earlier[1] + later[1])


def decay_prefix(values, rate_row):
    channels, length = values.shape
    block_len = min(128, length)
    block_count = length // block_len
    offsets = jnp.arange(block_len, dtype=jnp.float32)
    rising = jnp.exp(rate_row[:, None] * offsets[None, :])
    falling = jnp.exp(-rate_row[:, None] * offsets[None, :])
    shaped = values.reshape(channels, block_count, block_len) * rising[:, None, :]
    triangle = (offsets[:, None] <= offsets[None, :]).astype(jnp.float32)
    summed = jnp.einsum("cqs,st->cqt", shaped, triangle, precision=lax.Precision.HIGHEST)
    inside = summed * falling[:, None, :]
    factor = jnp.broadcast_to(jnp.exp(-rate_row * block_len)[:, None], (channels, block_count))
    _, running = lax.associative_scan(pair_combine, (factor, inside[:, :, -1]), axis=1)
    entering = jnp.concatenate([jnp.zeros((channels, 1), jnp.float32), running[:, :-1]], axis=1)
    carried = entering[:, :, None] * jnp.exp(
        -rate_row[:, None, None] * (offsets[None, None, :] + 1.0)
    )
    return (inside + carried).reshape(channels, length)


def modal_output(signal, rates, coeffs, starts):
    length = signal.shape[1]
    offsets = jnp.arange(length, dtype=jnp.float32)

    def one_mode(running_sum, params):
        rate_row, coeff_row, start_row = params
        states = decay_prefix(signal, rate_row) + start_row[:, None] * jnp.exp(
            -rate_row[:, None] * (offsets[None, :] + 1.0)
        )
        return (running_sum + coeff_row[:, None] * states, states)

    result, states_all = lax.scan(one_mode, jnp.zeros_like(signal), (rates, coeffs, starts))
    return (result, states_all)


def modal_grads(states_all, upstream, rates, coeffs, starts, finals):
    length = upstream.shape[1]
    offsets = jnp.arange(length, dtype=jnp.float32)

    def one_mode(running_sum, params):
        rate_row, coeff_row, start_row, final_row, states = params
        adjoint = jnp.flip(decay_prefix(jnp.flip(upstream, 1), rate_row), 1)
        adjoint = adjoint + final_row[:, None] * jnp.exp(
            -rate_row[:, None] * (length - offsets[None, :])
        )
        previous = jnp.concatenate([start_row[:, None], states[:, :-1]], axis=1)
        sums_pair = (jnp.sum(upstream * states, axis=1), jnp.sum(adjoint * previous, axis=1))
        return (running_sum + coeff_row[:, None] * adjoint, sums_pair)

    result, (alpha_rows, beta_rows) = lax.scan(
        one_mode, jnp.zeros_like(upstream), (rates, coeffs, starts, finals, states_all)
    )
    return (result, alpha_rows, beta_rows)


def coef_grads(alpha_rows, beta_rows, rates, residue):
    scales = jnp.sqrt(-jnp.expm1(-2.0 * rates))
    grad_res = scales * alpha_rows
    grad_log = rates * (
        alpha_rows * residue * jnp.exp(-2.0 * rates) / scales
        - jnp.exp(-rates) * residue * scales * beta_rows
    )
    return (grad_res, grad_log)


def local(features, short_taps, residue, decay_rate, w_out, cotangent):
    tok_count = features.shape[0]
    tap_reach = short_taps.shape[1] - 1
    earlier = shifted(features[tok_count - tap_reach :], "seq", 1)
    extended = jnp.concatenate([earlier, features], axis=0)
    mixed_in = short_taps[:, 0, :] * features
    for tap_index in range(1, tap_reach + 1):
        mixed_in = (
            mixed_in
            + short_taps[:, tap_index, :]
            * extended[tap_reach - tap_index : tap_reach - tap_index + tok_count]
        )
    query_part = mixed_in[:, 0, :]
    keyed = mixed_in[:, 1, :]
    valued = mixed_in[:, 2, :]
    product = (keyed * valued).astype(jnp.bfloat16)
    coeffs = residue * jnp.sqrt(-jnp.expm1(-2.0 * decay_rate))
    mode_count = residue.shape[0]
    chan_share = product.shape[1] // lax.axis_size("seq")
    first_channel = lax.axis_index("seq") * chan_share
    local_rates = lax.dynamic_slice_in_dim(decay_rate, first_channel, chan_share, 1)
    local_coeffs = lax.dynamic_slice_in_dim(coeffs, first_channel, chan_share, 1)
    local_residue = lax.dynamic_slice_in_dim(residue, first_channel, chan_share, 1)
    empty_state = jnp.zeros((mode_count, chan_share), jnp.float32)
    by_channel = lax.all_to_all(product.T, "seq", split_axis=0, concat_axis=1, tiled=True).astype(
        jnp.float32
    )
    conv_channels, mode_states = modal_output(by_channel, local_rates, local_coeffs, empty_state)
    convolved = lax.all_to_all(
        conv_channels.astype(jnp.bfloat16), "seq", split_axis=1, concat_axis=0, tiled=True
    ).T
    gated = (query_part * convolved).astype(jnp.bfloat16)
    full_weight = lax.all_gather(w_out, "seq", axis=1, tiled=True)
    partial_out = jnp.dot(gated, full_weight, preferred_element_type=jnp.float32)
    mixed = lax.psum_scatter(
        partial_out.astype(jnp.bfloat16), "tp", scatter_dimension=1, tiled=True
    )
    grad_rows = lax.all_gather(cotangent, "tp", axis=1, tiled=True)
    grad_gated = lax.dot_general(
        grad_rows, full_weight, (((1,), (1,)), ((), ())), preferred_element_type=jnp.float32
    ).astype(jnp.bfloat16)
    weight_term = lax.dot_general(
        gated, grad_rows, (((0,), (0,)), ((), ())), preferred_element_type=jnp.float32
    )
    grad_weight = lax.psum_scatter(weight_term, "seq", scatter_dimension=1, tiled=True)
    grad_conv = (grad_gated * query_part).astype(jnp.bfloat16)
    grad_channels = lax.all_to_all(
        grad_conv.T, "seq", split_axis=0, concat_axis=1, tiled=True
    ).astype(jnp.float32)
    back_channels, alpha_rows, beta_rows = modal_grads(
        mode_states, grad_channels, local_rates, local_coeffs, empty_state, empty_state
    )
    grad_product = lax.all_to_all(
        back_channels.astype(jnp.bfloat16), "seq", split_axis=1, concat_axis=0, tiled=True
    ).T
    local_res, local_log = coef_grads(alpha_rows, beta_rows, local_rates, local_residue)
    grad_residue, grad_log_rate = (
        lax.all_gather(local_res, "seq", axis=1, tiled=True),
        lax.all_gather(local_log, "seq", axis=1, tiled=True),
    )
    grad_query = grad_gated * convolved
    grad_key = (grad_product * valued).astype(jnp.bfloat16)
    grad_value = (grad_product * keyed).astype(jnp.bfloat16)
    grad_mixed_in = jnp.stack([grad_query, grad_key, grad_value], axis=1)
    later_rows = shifted(grad_mixed_in[:tap_reach], "seq", -1)
    grad_ext = jnp.concatenate([grad_mixed_in, later_rows], axis=0)
    grad_feat = short_taps[:, 0, :] * grad_mixed_in
    tap_terms = [
        jnp.einsum("tjc,tjc->jc", grad_mixed_in, features, preferred_element_type=jnp.float32)
    ]
    for tap_index in range(1, tap_reach + 1):
        grad_feat = (
            grad_feat + short_taps[:, tap_index, :] * grad_ext[tap_index : tap_index + tok_count]
        )
        tap_terms.append(
            jnp.einsum(
                "tjc,tjc->jc",
                grad_mixed_in,
                extended[tap_reach - tap_index : tap_reach - tap_index + tok_count],
                preferred_element_type=jnp.float32,
            )
        )
    tap_local = jnp.stack(tap_terms, axis=1)
    grad_taps = lax.psum(tap_local, "seq")
    return (
        mixed,
        grad_feat.astype(jnp.bfloat16),
        grad_weight,
        grad_taps,
        grad_residue,
        grad_log_rate,
    )


def solution(mesh):
    return jax.shard_map(
        local,
        mesh=mesh,
        in_specs=(
            P("seq", None, "tp"),
            P(None, None, "tp"),
            P(None, "tp"),
            P(None, "tp"),
            P("tp", "seq"),
            P("seq", "tp"),
        ),
        out_specs=(
            P("seq", "tp"),
            P("seq", None, "tp"),
            P("tp", "seq"),
            P(None, None, "tp"),
            P(None, "tp"),
            P(None, "tp"),
        ),
        check_vma=False,
    )
```

profile of v0, /device:TPU:0, one launch (start us, length us, event | category | flops | bytes accessed | tf_op | source)
XLA Modules:
  0.0 840.7 jit_solution(3258179935622488126)
XLA Ops:
  9.5 4.9 collective-permute-start
  16.1 7.5 multiply_add_fusion.13
  23.6 11.2 %all-gather.5.cloned.1.call-done = bf16[256,4096]{1,0:T(8,128)(2,1)} async-done(((bf16[256,1024]{1,0:T(8,128)(2,1)}), bf16[256,4096]{1,0:T(8,128)(2,1)}) %all-gather.5.cloned.1.call-update) | async-done | bytes 2097168 | tf_op jit(solution)/shard_map/all_gather | solution.py:119
  34.9 127.5 %all-gather.3.cloned.1.call-done = bf16[1024,4096]{1,0:T(8,128)(2,1)} async-done(((bf16[1024,512]{1,0:T(8,128)(2,1)}), bf16[1024,4096]{1,0:T(8,128)(2,1)}) %all-gather.3.cloned.1.call-update) | async-done | bytes 8388624 | tf_op jit(solution)/shard_map/all_gather | solution.py:114
  162.4 6.4 convolution_convert_fusion.1
  170.8 3.5 all-to-all-start
  175.1 1.9 copy.117
  177.1 11.5 %all-to-all-done = bf16[8,128,256]{1,2,0:T(8,128)(2,1)S(1)} async-done(((bf16[8,128,256]{1,2,0:T(8,128)(2,1)}), bf16[8,128,256]{1,2,0:T(8,128)(2,1)S(1)}, u32[]{:S(2)}, u32[]{:S(2)}) %all-to-all-start) | async-done | bytes 524320 | tf_op jit(solution)/shard_map/all_to_all | solution.py:106
  188.6 4.1 all-to-all-start.2
  193.1 87.9 %while.30 = (s32[]{:T(128)}, f32[128,2048]{0,1:T(8,128)}, f32[16,128,2048]{1,2,0:T(8,128)}, f32[16,128]{1,0:T(8,128)S(1)}, f32[128,2048]{1,0:T(8,128)S(1)}, /*in...) while((s32[]{:T(128)}, f32[128,2048]{0,1:T(8,128)}, ...), condition=%wide.region_1.2_spmd.clone.clone, body=%wide.region_0.1_spmd.clone.clone.sunk | while | flops 406142976 | bytes 10090643 | solution.py:48
  200.4 2.7 fusion.90
  205.9 2.7 fusion.90
  211.5 2.7 fusion.90
  217.0 2.7 fusion.90
  222.6 2.7 fusion.90
  228.1 2.7 fusion.90
  233.8 2.7 fusion.90
  239.4 2.7 fusion.90
  245.0 2.7 fusion.90
  250.5 2.7 fusion.90
  256.1 2.7 fusion.90
  261.7 2.7 fusion.90
  267.3 2.7 fusion.90
  272.8 2.7 fusion.90
  278.4 2.7 fusion.90
  282.1 110.4 %while.29 = (s32[]{:T(128)}, f32[128,2048]{0,1:T(8,128)}, f32[16,128]{1,0:T(8,128)S(1)}, f32[16,128]{1,0:T(8,128)S(1)}, f32[16,128]{1,0:T(8,128)S(1)}, /*index=5...) while((s32[]{:T(128)}, f32[128,2048]{0,1:T(8,128)}, ...), condition=%wide.region_6.7_spmd.clone, body=%wide.region_3.0_spmd.clone.sunk | while | flops 406404864 | bytes 18472624 | solution.py:66
  284.8 1.5 multiply_reduce_fusion.4
  290.6 1.5 multiply_reduce_fusion.4
  292.1 2.7 multiply_reduce_fusion.5
  297.6 1.5 multiply_reduce_fusion.4
  299.1 2.7 multiply_reduce_fusion.5
  304.6 1.5 multiply_reduce_fusion.4
  306.1 2.7 multiply_reduce_fusion.5
  311.5 1.5 multiply_reduce_fusion.4
  313.1 2.7 multiply_reduce_fusion.5
  318.5 1.5 multiply_reduce_fusion.4
  320.1 2.7 multiply_reduce_fusion.5
  327.0 2.7 multiply_reduce_fusion.5
  334.0 2.7 multiply_reduce_fusion.5
  339.4 1.5 multiply_reduce_fusion.4
  341.0 2.7 multiply_reduce_fusion.5
  348.0 2.7 multiply_reduce_fusion.5
  354.9 2.7 multiply_reduce_fusion.5
  361.9 2.7 multiply_reduce_fusion.5
  368.9 2.7 multiply_reduce_fusion.5
  374.3 1.5 multiply_reduce_fusion.4
  375.9 2.7 multiply_reduce_fusion.5
  382.9 2.7 multiply_reduce_fusion.5
  389.8 2.7 multiply_reduce_fusion.5
  392.6 2.2 convert_element_type.132
  394.8 5.9 all-to-all-start.3
  401.5 12.4 %all-to-all-done.3 = bf16[128,8,256]{0,2,1:T(8,128)(2,1)S(1)} async-done(((bf16[128,8,256]{0,2,1:T(8,128)(2,1)}), bf16[128,8,256]{0,2,1:T(8,128)(2,1)S(1)}, u32[]{:S(2)}, u32[]{:S(2)}) %all-to-all-start.3) | async-done | bytes 524320 | tf_op jit(solution)/shard_map/all_to_all | solution.py:134
  413.9 4.1 all-to-all-start.1
  418.3 2.8 fusion.46
  421.0 10.4 %all-to-all-done.1 = bf16[128,8,256]{0,2,1:T(8,128)(2,1)} async-done(((bf16[128,8,256]{0,2,1:T(8,128)(2,1)}), bf16[128,8,256]{0,2,1:T(8,128)(2,1)}, u32[]{:S(2)}, u32[]{:S(2)}) %all-to-all-start.1) | async-done | bytes 524320 | tf_op jit(solution)/shard_map/all_to_all | solution.py:110
  433.5 8.9 %fusion.31 = (f32[3,1024]{1,0:T(4,128)S(1)}, f32[3,1024]{1,0:T(4,128)S(1)}, f32[3,1024]{1,0:T(4,128)S(1)}, f32[3,1024]{1,0:T(4,128)S(1)}, f32[3,1024]{1,0:T(4,12...) fusion(bf16[256,3,1024]{2,0,1:T(8,128)(2,1)} %param.10, bf16[6,3,1024]{2,0,1:T(8,128)(2,1)S(1)} %collective-permute-done, ...), kind=kLoop, calls=%fused_computation.97 | loop fusion | flops 40872960 | bytes 3268608 | tf_op jit(solution)/shard_map/tjc,tjc->jc/dot_general | solution.py:157
  443.3 7.3 convolution_convert_fusion
  450.6 9.9 %fusion.51 = f32[1024,4096]{1,0:T(8,128)} fusion(bf16[256,4096]{1,0:T(8,128)(2,1)} %all-gather.5.cloned.1.call-done, f32[256,3,1024]{2,0,1:T(8,128)S(1)} %copy-done.2, bf16[128,8,256]{0,2,1:T(8,128)(2,1)} %all-to-all-done.1), kind=kOutput, calls=%fused_computation.151 | convolution fusion | flops 2148270080 | bytes 20447232 | tf_op jit(solution)/shard_map/dot_general | solution.py:123
  463.4 30.8 %all_gather.14 = f32[16,1024]{1,0:T(8,128)S(1)} all-gather(f32[16,128]{1,0:T(8,128)S(1)} %get-tuple-element.270), channel_id=1, replica_groups=mesh['seq'=8,'tp'=4] {'seq'}, dimensions={1}, use_global_device_ids=true | all-gather | bytes 73728 | tf_op jit(solution)/shard_map/all_gather | solution.py:139
  494.2 30.5 %all_gather.15 = f32[16,1024]{1,0:T(8,128)S(1)} all-gather(f32[16,128]{1,0:T(8,128)S(1)} %get-tuple-element.269), channel_id=1, replica_groups=mesh['seq'=8,'tp'=4] {'seq'}, dimensions={1}, use_global_device_ids=true | all-gather | bytes 73728 | tf_op jit(solution)/shard_map/all_gather | solution.py:140
  524.8 3.7 add_convert_fusion
  528.6 1.6 copy.32
  530.2 15.9 %reduce-scatter.3.cloned.1.call-done = bf16[256,1024]{1,0:T(8,128)(2,1)} async-done(((bf16[256,4096]{1,0:T(8,128)(2,1)}), bf16[256,1024]{1,0:T(8,128)(2,1)}) %reduce-scatter.3.cloned.1.call-update) | async-done | bytes 524304 | tf_op jit(solution)/shard_map/reduce_scatter | solution.py:116
  546.0 286.8 %reduce-scatter.5.cloned.1.call-done = f32[1024,512]{1,0:T(8,128)} async-done(((f32[1024,4096]{1,0:T(8,128)}), f32[1024,512]{1,0:T(8,128)}) %reduce-scatter.5.cloned.1.call-update) | async-done | bytes 2097168 | tf_op jit(solution)/shard_map/reduce_scatter | solution.py:126
  (1451 shorter events, 116.9 us)
Async XLA Ops:
  7.2 27.7 %all-gather.5.cloned.1.call-start = ((), (), s32[]{:S(2)}) async-start(), calls=%async_computation.8 | async-start | bytes 2621440 | tf_op jit(solution)/shard_map/all_gather | solution.py:119
  7.9 154.5 %all-gather.3.cloned.1.call-start = ((), (), s32[]{:S(2)}) async-start(), calls=%async_computation.6 | async-start | bytes 9437184 | tf_op jit(solution)/shard_map/all_gather | solution.py:114
  9.5 6.6 collective-permute-start
  23.6 145.1 %copy-start.1 = (f32[256,3,1024]{2,0,1:T(8,128)}, f32[256,3,1024]{2,0,1:T(8,128)S(1)}, u32[]{:S(2)}) copy-start(f32[256,3,1024]{2,0,1:T(8,128)S(1)} %multiply_add_fusion.13) | copy-start | bytes 9437188
  168.7 1.2 copy-start.7
  170.8 17.7 %all-to-all-start = ((bf16[8,128,256]{1,2,0:T(8,128)(2,1)}), bf16[8,128,256]{1,2,0:T(8,128)(2,1)S(1)}, u32[]{:S(2)}, u32[]{:S(2)}) async-start(bf16[8,128,256]{1,2,0:T(8,128)(2,1)} %bitcast.237), calls=%async_computation | async-start | bytes 1048576 | tf_op jit(solution)/shard_map/all_to_all | solution.py:106
  188.6 92.5 %all-to-all-start.2 = ((bf16[8,128,256]{1,2,0:T(8,128)(2,1)}), bf16[8,128,256]{1,2,0:T(8,128)(2,1)}, u32[]{:S(2)}, u32[]{:S(2)}) async-start(bf16[8,128,256]{1,2,0:T(8,128)(2,1)} %bitcast.236), calls=%async_computation.3 | async-start | bytes 1048576 | tf_op jit(solution)/shard_map/all_to_all | solution.py:128
  392.6 8.1 copy-start
  394.8 19.1 %all-to-all-start.3 = ((bf16[128,8,256]{0,2,1:T(8,128)(2,1)}), bf16[128,8,256]{0,2,1:T(8,128)(2,1)S(1)}, u32[]{:S(2)}, u32[]{:S(2)}) async-start(bf16[128,8,256]{0,2,1:T(8,128)(2,1)} %bitcast.27), calls=%async_computation.4 | async-start | bytes 1048576 | tf_op jit(solution)/shard_map/all_to_all | solution.py:134
  413.9 17.5 %all-to-all-start.1 = ((bf16[128,8,256]{0,2,1:T(8,128)(2,1)}), bf16[128,8,256]{0,2,1:T(8,128)(2,1)}, u32[]{:S(2)}, u32[]{:S(2)}) async-start(bf16[128,8,256]{0,2,1:T(8,128)(2,1)} %bitcast.20), calls=%async_computation.1 | async-start | bytes 1048576 | tf_op jit(solution)/shard_map/all_to_all | solution.py:110
  418.0 110.5 %all-reduce.21.cloned.1.call-start = ((), (), s32[]{:S(2)}) async-start(), calls=%async_computation.10 | async-start | bytes 229376 | tf_op jit(solution)/shard_map/psum | solution.py:165
  421.0 22.2 %copy-start.2 = (f32[256,3,1024]{2,0,1:T(8,128)S(1)}, f32[256,3,1024]{2,0,1:T(8,128)}, u32[]{:S(2)}) copy-start(f32[256,3,1024]{2,0,1:T(8,128)} %copy-done.1) | copy-start | bytes 9437188
  432.7 0.8 copy-start.5
  442.5 0.7 copy-start.8
  443.2 102.8 %reduce-scatter.3.cloned.1.call-start = ((), (), s32[]{:S(2)}) async-start(), calls=%async_computation.7 | async-start | bytes 2621440 | tf_op jit(solution)/shard_map/reduce_scatter | solution.py:116
  450.6 382.3 %reduce-scatter.5.cloned.1.call-start = ((), (), s32[]{:S(2)}) async-start(), calls=%async_computation.9 | async-start | bytes 18874368 | tf_op jit(solution)/shard_map/reduce_scatter | solution.py:126
  460.5 1.1 copy-start.3
  460.5 1.2 copy-start.4
  460.5 1.4 copy-start.6
  462.1 62.6 %collective-permute-start.1 = (bf16[6,3,1024]{2,0,1:T(8,128)(2,1)S(1)}, bf16[6,3,1024]{2,0,1:T(8,128)(2,1)S(1)}, u32[]{:S(2)}, u32[]{:S(2)}) collective-permute-start(bf16[6,3,1024]{2,0,1:T(8,128)(2,1)S(1)} %slice.365), channel_id=1, source_target_pairs={{4,0},{8,4},{12,8},{16,12},{20,16},{24,20},{28,24},{5,1},{9,5},{13... | collective-permute-start | bytes 110600 | tf_op jit(solution)/shard_map/ppermute | solution.py:10
Sparse Core Ops, SparseCore 0:
  9.6 25.2 all-gather.4
  36.9 125.3 all-gather.2
  443.3 68.2 all-reduce.20
  514.7 31.2 reduce-scatter.2
  550.2 282.5 reduce-scatter.4
where the time goes:
time: 843 us; the launch traced here: 841 us
  waiting for transfers between devices  477 us (57%)
  other arithmetic  175 us (21%)
  blocking collectives  61.3 us (7%)
  matrix products  46.8 us (6%)
  local copies, waits for them, and re-layouts  36.4 us (4%)
  starting transfers between devices  24.2 us (3%)
  between operations  14.1 us (2%)
    reduce_scatter x1, waiting for transfers between devices, local(): lax.psum_scatter(weight_term, 'seq', scatter_dimension=1, tiled=True)  287 us
    all_gather x1, waiting for transfers between devices, local(): full_weight = lax.all_gather(w_out, 'seq', axis=1, tiled=True)  127 us
    reduce_sum x16, other arithmetic, one_mode(): jnp.sum(adjoint * previous, axis=1)  41.6 us
    add x16, other arithmetic, one_mode(): return (running_sum + coeff_row[:, None] * states, states)  41.3 us
    all_gather x1, blocking collectives, local(): lax.all_gather(local_res, 'seq', axis=1, tiled=True)  30.8 us
    all_gather x1, blocking collectives, local(): lax.all_gather(local_log, 'seq', axis=1, tiled=True)  30.5 us
    reduce_sum x16, other arithmetic, one_mode(): jnp.sum(upstream * states, axis=1)  24.3 us
    dot_general x32, matrix products, decay_prefix(): jnp.einsum('cqs,st->cqt', shaped, triangle, precision=lax.Precision.HIGHEST)  23.3 us
  transfers between devices with their start and end apart: 11, of which 8 were waited for; matrix products, arithmetic and copies ran while one was open for 15% of the time, Pallas kernels for 0%

commit v1 on v0

v1 whole, which is shorter than its diff:
```python
import jax
import jax.numpy as jnp
from jax import lax
from jax.experimental import pallas as pl
from jax.experimental.pallas import tpu as pltpu
from jax.sharding import PartitionSpec as P


def shifted(array, axis, by):
    devices = lax.axis_size(axis)
    pairs = [(i, i + by) for i in range(devices) if 0 <= i + by < devices]
    return lax.ppermute(array, axis, pairs)


GROUP = 16


def token_block(tokens):
    return min(256, tokens)


def row_total(terms):
    return jnp.sum(terms, axis=0, keepdims=True)


def forward_kernel(x_ref, decay_ref, coeff_ref, out_ref, entry_ref, state_ref):
    @pl.when(pl.program_id(0) == 0)
    def _():
        state_ref[...] = jnp.zeros_like(state_ref)

    entry_ref[0] = state_ref[...]
    decay = decay_ref[...]
    coeff = coeff_ref[...]

    def step(group, state):
        rows = pl.ds(pl.multiple_of(group * GROUP, GROUP), GROUP)
        x_rows = x_ref[rows, :].astype(jnp.float32)
        outs = []
        for j in range(GROUP):
            state = decay * state + x_rows[j : j + 1, :]
            outs.append(row_total(coeff * state))
        out_ref[rows, :] = jnp.concatenate(outs, axis=0).astype(out_ref.dtype)
        return state

    state_ref[...] = lax.fori_loop(0, x_ref.shape[0] // GROUP, step, state_ref[...])


def backward_kernel(
    x_ref, g_ref, entry_ref, decay_ref, coeff_ref, out_ref, alpha_ref, beta_ref, adj_ref, before_ref
):
    @pl.when(pl.program_id(0) == 0)
    def _():
        adj_ref[...] = jnp.zeros_like(adj_ref)
        alpha_ref[...] = jnp.zeros_like(alpha_ref)
        beta_ref[...] = jnp.zeros_like(beta_ref)

    decay = decay_ref[...]
    coeff = coeff_ref[...]
    groups = x_ref.shape[0] // GROUP

    def states(group, carry):
        state, alpha = carry
        first = pl.multiple_of(group * GROUP, GROUP)
        x_rows = x_ref[pl.ds(first, GROUP), :].astype(jnp.float32)
        g_rows = g_ref[pl.ds(first, GROUP), :].astype(jnp.float32)
        for j in range(GROUP):
            before_ref[first + j] = state
            state = decay * state + x_rows[j : j + 1, :]
            alpha = alpha + g_rows[j : j + 1, :] * state
        return (state, alpha)

    _, alpha = lax.fori_loop(0, groups, states, (entry_ref[0], alpha_ref[...]))
    alpha_ref[...] = alpha

    def adjoints(index, carry):
        adjoint, beta = carry
        first = pl.multiple_of((groups - 1 - index) * GROUP, GROUP)
        g_rows = g_ref[pl.ds(first, GROUP), :].astype(jnp.float32)
        outs = [None] * GROUP
        for j in range(GROUP - 1, -1, -1):
            adjoint = decay * adjoint + g_rows[j : j + 1, :]
            beta = beta + adjoint * before_ref[first + j]
            outs[j] = row_total(coeff * adjoint)
        out_ref[pl.ds(first, GROUP), :] = jnp.concatenate(outs, axis=0).astype(out_ref.dtype)
        return (adjoint, beta)

    adjoint, beta = lax.fori_loop(0, groups, adjoints, (adj_ref[...], beta_ref[...]))
    adj_ref[...] = adjoint
    beta_ref[...] = beta


def modal_output(signal, decay, coeffs):
    tokens, channels = signal.shape
    modes = decay.shape[0]
    block = token_block(tokens)
    blocks = tokens // block
    fixed = pl.BlockSpec((modes, channels), lambda i: (0, 0))
    return pl.pallas_call(
        forward_kernel,
        grid=(blocks,),
        in_specs=[pl.BlockSpec((block, channels), lambda i: (i, 0)), fixed, fixed],
        out_specs=[
            pl.BlockSpec((block, channels), lambda i: (i, 0)),
            pl.BlockSpec((1, modes, channels), lambda i: (i, 0, 0)),
        ],
        out_shape=[
            jax.ShapeDtypeStruct((tokens, channels), jnp.bfloat16),
            jax.ShapeDtypeStruct((blocks, modes, channels), jnp.float32),
        ],
        scratch_shapes=[pltpu.VMEM((modes, channels), jnp.float32)],
        cost_estimate=pl.CostEstimate(
            flops=tokens * modes * channels * 3000,
            bytes_accessed=tokens * channels * 4,
            transcendentals=0,
        ),
        name="modal_forward",
    )(signal, decay, coeffs)


def modal_grads(signal, upstream, entries, decay, coeffs):
    tokens, channels = signal.shape
    modes = decay.shape[0]
    block = token_block(tokens)
    blocks = tokens // block
    fixed = pl.BlockSpec((modes, channels), lambda i: (0, 0))
    rows = pl.BlockSpec((block, channels), lambda i: (blocks - 1 - i, 0))
    return pl.pallas_call(
        backward_kernel,
        grid=(blocks,),
        in_specs=[
            rows,
            rows,
            pl.BlockSpec((1, modes, channels), lambda i: (blocks - 1 - i, 0, 0)),
            fixed,
            fixed,
        ],
        out_specs=[rows, fixed, fixed],
        out_shape=[
            jax.ShapeDtypeStruct((tokens, channels), jnp.bfloat16),
            jax.ShapeDtypeStruct((modes, channels), jnp.float32),
            jax.ShapeDtypeStruct((modes, channels), jnp.float32),
        ],
        scratch_shapes=[
            pltpu.VMEM((modes, channels), jnp.float32),
            pltpu.VMEM((block, modes, channels), jnp.float32),
        ],
        cost_estimate=pl.CostEstimate(
            flops=tokens * modes * channels * 5000,
            bytes_accessed=tokens * channels * 6,
            transcendentals=0,
        ),
        name="modal_backward",
    )(signal, upstream, entries, decay, coeffs)


def coef_grads(alpha_rows, beta_rows, rates, residue):
    scales = jnp.sqrt(-jnp.expm1(-2.0 * rates))
    grad_res = scales * alpha_rows
    grad_log = rates * (
        alpha_rows * residue * jnp.exp(-2.0 * rates) / scales
        - jnp.exp(-rates) * residue * scales * beta_rows
    )
    return (grad_res, grad_log)


def local(features, short_taps, residue, decay_rate, w_out, cotangent):
    tok_count = features.shape[0]
    tap_reach = short_taps.shape[1] - 1
    earlier = shifted(features[tok_count - tap_reach :], "seq", 1)
    extended = jnp.concatenate([earlier, features], axis=0)
    mixed_in = short_taps[:, 0, :] * features
    for tap_index in range(1, tap_reach + 1):
        mixed_in = (
            mixed_in
            + short_taps[:, tap_index, :]
            * extended[tap_reach - tap_index : tap_reach - tap_index + tok_count]
        )
    query_part = mixed_in[:, 0, :]
    keyed = mixed_in[:, 1, :]
    valued = mixed_in[:, 2, :]
    product = (keyed * valued).astype(jnp.bfloat16)
    coeffs = residue * jnp.sqrt(-jnp.expm1(-2.0 * decay_rate))
    mode_count = residue.shape[0]
    chan_share = product.shape[1] // lax.axis_size("seq")
    first_channel = lax.axis_index("seq") * chan_share
    local_rates = lax.dynamic_slice_in_dim(decay_rate, first_channel, chan_share, 1)
    local_coeffs = lax.dynamic_slice_in_dim(coeffs, first_channel, chan_share, 1)
    local_residue = lax.dynamic_slice_in_dim(residue, first_channel, chan_share, 1)
    local_decay = jnp.exp(-local_rates)
    seq_count = lax.axis_size("seq")
    full_weight = lax.all_gather(w_out, "seq", axis=1, tiled=True)
    grad_rows = lax.all_gather(cotangent, "tp", axis=1, tiled=True)
    by_channel = lax.all_to_all(product, "seq", split_axis=1, concat_axis=0, tiled=True)
    conv_channels, entries = modal_output(by_channel, local_decay, local_coeffs)
    convolved = lax.all_to_all(conv_channels, "seq", split_axis=0, concat_axis=1, tiled=True)
    gated = (query_part * convolved).astype(jnp.bfloat16)
    quarter = lax.all_to_all(cotangent, "tp", split_axis=0, concat_axis=1, tiled=True)
    quarter = lax.all_to_all(quarter, "seq", split_axis=1, concat_axis=0, tiled=True)
    full_weight, gated, quarter = lax.optimization_barrier((full_weight, gated, quarter))
    half = gated.shape[1] // 2
    gated_first = lax.all_gather(gated[:, :half], "seq", axis=0, tiled=True)
    gated_second = lax.all_gather(gated[:, half:], "seq", axis=0, tiled=True)
    cot_columns = lax.all_gather(quarter, "tp", axis=0)
    grad_gated = lax.dot_general(
        grad_rows, full_weight, (((1,), (1,)), ((), ())), preferred_element_type=jnp.float32
    ).astype(jnp.bfloat16)
    grad_conv = (grad_gated * query_part).astype(jnp.bfloat16)
    partial_out = jnp.dot(gated, full_weight, preferred_element_type=jnp.float32).astype(
        jnp.bfloat16
    )
    grad_conv, partial_out = lax.optimization_barrier((grad_conv, partial_out))
    mixed = lax.psum_scatter(partial_out, "tp", scatter_dimension=1, tiled=True)
    grad_channels = lax.all_to_all(grad_conv, "seq", split_axis=1, concat_axis=0, tiled=True)
    back_channels, alpha_rows, beta_rows = modal_grads(
        by_channel, grad_channels, entries, local_decay, local_coeffs
    )
    local_res, local_log = coef_grads(alpha_rows, beta_rows, local_rates, local_residue)
    mode_rows = jnp.concatenate([local_res, local_log], axis=0).astype(jnp.bfloat16)
    sent = jnp.concatenate(
        [
            back_channels.reshape(seq_count, tok_count, chan_share),
            jnp.broadcast_to(mode_rows, (seq_count, 2 * mode_count, chan_share)),
        ],
        axis=1,
    )
    received = lax.all_to_all(sent, "seq", split_axis=0, concat_axis=0, tiled=True)
    received, gated_first, cot_columns = lax.optimization_barrier(
        (received, gated_first, cot_columns)
    )
    received = received.transpose(1, 0, 2).reshape(tok_count + 2 * mode_count, -1)
    grad_product = received[:tok_count]
    grad_residue = received[tok_count : tok_count + mode_count].astype(jnp.float32)
    grad_log_rate = received[tok_count + mode_count :].astype(jnp.float32)
    grad_query = grad_gated * convolved
    grad_key = (grad_product * valued).astype(jnp.bfloat16)
    grad_value = (grad_product * keyed).astype(jnp.bfloat16)
    grad_mixed_in = jnp.stack([grad_query, grad_key, grad_value], axis=1)
    later_rows = shifted(grad_mixed_in[:tap_reach], "seq", -1)
    grad_ext = jnp.concatenate([grad_mixed_in, later_rows], axis=0)
    grad_feat = short_taps[:, 0, :] * grad_mixed_in
    tap_terms = [
        jnp.einsum("tjc,tjc->jc", grad_mixed_in, features, preferred_element_type=jnp.float32)
    ]
    for tap_index in range(1, tap_reach + 1):
        grad_feat = (
            grad_feat + short_taps[:, tap_index, :] * grad_ext[tap_index : tap_index + tok_count]
        )
        tap_terms.append(
            jnp.einsum(
                "tjc,tjc->jc",
                grad_mixed_in,
                extended[tap_reach - tap_index : tap_reach - tap_index + tok_count],
                preferred_element_type=jnp.float32,
            )
        )
    tap_local = jnp.stack(tap_terms, axis=1)
    grad_taps = lax.psum(tap_local, "seq")
    tp_count = lax.axis_size("tp")
    cot_columns = (
        cot_columns.reshape(tp_count, seq_count, tok_count // tp_count, -1)
        .transpose(1, 0, 2, 3)
        .reshape(seq_count * tok_count, -1)
    )
    grad_feat = grad_feat.astype(jnp.bfloat16)
    gated_second, _ = lax.optimization_barrier((gated_second, grad_feat))
    grad_weight = jnp.concatenate(
        [
            lax.dot_general(
                rows, cot_columns, (((0,), (0,)), ((), ())), preferred_element_type=jnp.float32
            )
            for rows in (gated_first, gated_second)
        ],
        axis=0,
    )
    return (
        mixed,
        grad_feat,
        grad_weight,
        grad_taps,
        grad_residue,
        grad_log_rate,
    )


def solution(mesh):
    return jax.shard_map(
        local,
        mesh=mesh,
        in_specs=(
            P("seq", None, "tp"),
            P(None, None, "tp"),
            P(None, "tp"),
            P(None, "tp"),
            P("tp", "seq"),
            P("seq", "tp"),
        ),
        out_specs=(
            P("seq", "tp"),
            P("seq", None, "tp"),
            P("tp", "seq"),
            P(None, None, "tp"),
            P(None, "tp"),
            P(None, "tp"),
        ),
        check_vma=False,
    )
```

time: 843 us -> 440 us (0.52)
  waiting for transfers between devices: 477 us -> 294 us
  other arithmetic: 175 us -> 29.6 us
  blocking collectives: 61.3 us -> 0 us
  matrix products: 46.8 us -> 19.2 us
  Pallas kernels: 0 us -> 22 us
  local copies, waits for them, and re-layouts: 36.4 us -> 20.2 us
  starting transfers between devices: 24.2 us -> 39.1 us
    reduce_scatter x2 -> x1, waiting for transfers between devices: 303 us -> 32.9 us  [local(): mixed = lax.psum_scatter(partial_out, 'tp', scatter_dimension=1, tiled=True)]
    all_gather x1, waiting for transfers between devices: 127 us -> 30.4 us  [local(): full_weight = lax.all_gather(w_out, 'seq', axis=1, tiled=True)]
    all_to_all x4 -> x6, waiting for transfers between devices: 34.2 us -> 113 us  [the longest x1 24.9 us: local(): lax.all_to_all(conv_channels, 'seq', split_axis=0, concat_axis=1, tiled=T...]
    reduce_sum x32 -> x0, other arithmetic: 65.9 us -> none  [the longest x16 41.6 us: one_mode(): jnp.sum(adjoint * previous, axis=1)]
    psum x1, waiting for transfers between devices: 0.01 us -> 65.8 us  [local(): grad_taps = lax.psum(tap_local, 'seq')]
    all_gather x2 -> x0, blocking collectives: 61.3 us -> none  [the longest x1 30.8 us: local(): lax.all_gather(local_res, 'seq', axis=1, tiled=True)]
    add x384 -> x0, other arithmetic: 47.6 us -> none  [the longest x16 41.3 us: one_mode(): return (running_sum + coeff_row[:, None] * states, states)]
    all_gather x0 -> x3, waiting for transfers between devices: none -> 31.9 us  [the longest x1 26.7 us: local(): gated_second = lax.all_gather(gated[:, half:], 'seq', axis=0, tiled=True)]
  transfers between devices with their start and end apart: 11 -> 15, of which waited for: 8 -> 14; matrix products, arithmetic and copies ran while one was open for 15% -> 15% of each run, Pallas kernels for 0% -> 5%
where the time goes in v1:
time: 440 us; the launch traced here: 438 us
  waiting for transfers between devices  294 us (67%)
  starting transfers between devices  39.1 us (9%)
  other arithmetic  29.6 us (7%)
  Pallas kernels  22 us (5%)
  local copies, waits for them, and re-layouts  20.2 us (5%)
  matrix products  19.2 us (4%)
  between operations  14.5 us (3%)
    psum x1, waiting for transfers between devices, local(): grad_taps = lax.psum(tap_local, 'seq')  65.8 us
    reduce_scatter x1, waiting for transfers between devices, local(): mixed = lax.psum_scatter(partial_out, 'tp', scatter_dimension=1, tiled=True)  32.9 us
    all_gather x1, waiting for transfers between devices, local(): full_weight = lax.all_gather(w_out, 'seq', axis=1, tiled=True)  30.4 us
    all_gather x1, waiting for transfers between devices, local(): gated_second = lax.all_gather(gated[:, half:], 'seq', axis=0, tiled=True)  26.7 us
    all_to_all x1, waiting for transfers between devices, local(): lax.all_to_all(conv_channels, 'seq', split_axis=0, concat_axis=1, tiled=T...  24.9 us
    all_to_all x1, waiting for transfers between devices, local(): lax.all_to_all(quarter, 'seq', split_axis=1, concat_axis=0, tiled=True)  24.8 us
    all_to_all x1, waiting for transfers between devices, local(): lax.all_to_all(sent, 'seq', split_axis=0, concat_axis=0, tiled=True)  24.7 us
    all_to_all x1, waiting for transfers between devices, local(): lax.all_to_all(product, 'seq', split_axis=1, concat_axis=0, tiled=True)  24.3 us
  transfers between devices with their start and end apart: 15, of which 14 were waited for; matrix products, arithmetic and copies ran while one was open for 15% of the time, Pallas kernels for 5%

profile of v1, /device:TPU:0, one launch (start us, length us, event | category | flops | bytes accessed | tf_op | source)
XLA Modules:
  0.0 438.4 jit_solution(9746200228286691502)
XLA Ops:
  7.2 0.7 all-gather.7.cloned.1.call-update
  7.9 0.8 slice.105
  8.7 4.9 %collective-permute-start = (bf16[6,3,1024]{2,0,1:T(8,128)(2,1)S(1)}, bf16[6,3,1024]{2,0,1:T(8,128)(2,1)S(1)}, u32[]{:S(2)}, u32[]{:S(2)}) collective-permute-start(bf16[6,3,1024]{2,0,1:T(8,128)(2,1)S(1)} %slice.105), channel_id=1, source_target_pairs={{0,4},{4,8},{8,12},{12,16},{16,20},{20,24},{24,28},{1,5},{5,9},{9,... | collective-permute-start | bytes 110600 | tf_op jit(solution)/shard_map/ppermute | solution.py:12
  13.6 1.5 fusion.18
  15.2 0.2 collective-permute-done
  15.3 7.4 %multiply_add_fusion = f32[256,3,1024]{2,0,1:T(8,128)S(1)} fusion(bf16[256,3,1024]{2,0,1:T(8,128)(2,1)} %param.6, bf16[6,3,1024]{2,0,1:T(8,128)(2,1)S(1)} %collective-permute-done, f32[3,1024]{1,0:T(4,128)S(1)} %get-tuple-element.82, f32[3,1024]{1,0:T(4,128)S(1)} %get-tuple-element.83, f32[3,1024]{1,0:T(4,128)S(1)} %get-tuple-element.84, ...), kind=kLoop, calls=%fused_computation.21 | loop fusion | flops 29884416 | bytes 4841472 | tf_op jit(solution)/shard_map/add | solution.py:174
  22.8 0.2 fusion.14
  23.0 0.1 copy.107
  23.1 0.9 copy.37
  23.9 6.7 %all-to-all-start = ((bf16[256,8,128]{2,0,1:T(8,128)(2,1)}), bf16[256,8,128]{2,0,1:T(8,128)(2,1)}, u32[]{:S(2)}, u32[]{:S(2)}) async-start(bf16[256,8,128]{2,0,1:T(8,128)(2,1)} %copy.37), calls=%async_computation | async-start | bytes 1048576 | tf_op jit(solution)/shard_map/all_to_all | solution.py:193
  30.6 0.7 all-gather.9.cloned.1.call-update
  31.4 1.3 fusion.16
  32.7 24.3 %all-to-all-done = bf16[256,8,128]{2,0,1:T(8,128)(2,1)} async-done(((bf16[256,8,128]{2,0,1:T(8,128)(2,1)}), bf16[256,8,128]{2,0,1:T(8,128)(2,1)}, u32[]{:S(2)}, u32[]{:S(2)}) %all-to-all-start) | async-done | bytes 524320 | tf_op jit(solution)/shard_map/all_to_all | solution.py:193
  57.0 4.1 all-to-all-start.2
  61.1 8.1 %modal_forward.1 = (bf16[2048,128]{1,0:T(8,128)(2,1)}, f32[8,16,128]{2,1,0:T(8,128)}) custom-call(bf16[2048,128]{1,0:T(8,128)(2,1)} %bitcast.16.x_ref, f32[16,128]{1,0:T(8,128)} %get-tuple-element.79.decay_ref, f32[16,128]{1,0:T(8,128)} %get-tuple-element.78.coeff_ref), custom_call_target="tpu_custom_call" | custom-call | flops 12582912000 | bytes 1048576 | tf_op jit(solution)/shard_map/modal_forward/pallas_call | solution.py:98
  69.2 0.8 all-to-all-done.2
  70.0 7.8 %all-to-all-start.1 = ((bf16[8,256,128]{2,1,0:T(8,128)(2,1)}), bf16[8,256,128]{2,1,0:T(8,128)(2,1)}, u32[]{:S(2)}, u32[]{:S(2)}) async-start(bf16[8,256,128]{2,1,0:T(8,128)(2,1)} %bitcast.133), calls=%async_computation.1 | async-start | bytes 1048576 | tf_op jit(solution)/shard_map/all_to_all | solution.py:195
  77.8 2.3 copy.39
  80.1 2.0 all_to_all.79
  82.0 2.0 copy.40
  84.0 24.9 %all-to-all-done.1 = bf16[8,256,128]{2,1,0:T(8,128)(2,1)} async-done(((bf16[8,256,128]{2,1,0:T(8,128)(2,1)}), bf16[8,256,128]{2,1,0:T(8,128)(2,1)}, u32[]{:S(2)}, u32[]{:S(2)}) %all-to-all-start.1) | async-done | bytes 524320 | tf_op jit(solution)/shard_map/all_to_all | solution.py:195
  109.0 4.2 all-to-all-start.3
  113.2 2.0 multiply_convert_fusion.3
  115.1 24.8 %all-to-all-done.3 = bf16[64,8,512]{2,0,1:T(8,128)(2,1)} async-done(((bf16[64,8,512]{2,0,1:T(8,128)(2,1)}), bf16[64,8,512]{2,0,1:T(8,128)(2,1)}, u32[]{:S(2)}, u32[]{:S(2)}) %all-to-all-start.3) | async-done | bytes 524320 | tf_op jit(solution)/shard_map/all_to_all | solution.py:198
  139.9 30.4 %all-gather.7.cloned.1.call-done = bf16[1024,4096]{1,0:T(8,128)(2,1)} async-done(((bf16[1024,512]{1,0:T(8,128)(2,1)}), bf16[1024,4096]{1,0:T(8,128)(2,1)}) %all-gather.7.cloned.1.call-update) | async-done | bytes 8388624 | tf_op jit(solution)/shard_map/all_gather | solution.py:191
  170.3 7.3 %convolution_convert_fusion = bf16[256,4096]{1,0:T(8,128)(2,1)} fusion(bf16[256,1024]{1,0:T(8,128)(2,1)} %multiply_convert_fusion.3, bf16[1024,4096]{1,0:T(8,128)(2,1)} %all-gather.7.cloned.1.call-done), kind=kOutput, calls=%fused_computation.7 | convolution fusion | flops 2148532224 | bytes 11010048 | tf_op jit(solution)/shard_map/dot_general | solution.py:208
  177.6 16.4 %all-gather.9.cloned.1.call-done = bf16[256,4096]{1,0:T(8,128)(2,1)} async-done(((bf16[256,1024]{1,0:T(8,128)(2,1)}), bf16[256,4096]{1,0:T(8,128)(2,1)}) %all-gather.9.cloned.1.call-update) | async-done | bytes 2097168 | tf_op jit(solution)/shard_map/all_gather | solution.py:192
  194.1 7.1 %multiply_convert_fusion.2 = (bf16[256,1024]{1,0:T(8,128)(2,1)S(1)}, bf16[256,1024]{1,0:T(8,128)(2,1)}) fusion(f32[256,3,1024]{2,0,1:T(8,128)S(1)} %multiply_add_fusion, bf16[1024,4096]{1,0:T(8,128)(2,1)} %all-gather.7.cloned.1.call-done, bf16[256,4096]{1,0:T(8,128)(2,1)} %all-gather.9.cloned.1.call-done), kind=kOutput, calls=%fused_computation.37 | convolution fusion | flops 2148532224 | bytes 12582912 | tf_op jit(solution)/shard_map/dot_general | solution.py:204
  201.2 0.9 copy_bitcast_fusion
  202.1 5.5 %all-to-all-start.4 = ((bf16[256,8,128]{2,0,1:T(8,128)(2,1)}), bf16[256,8,128]{2,0,1:T(8,128)(2,1)}, u32[]{:S(2)}, u32[]{:S(2)}) async-start(bf16[256,8,128]{2,0,1:T(8,128)(2,1)} %copy_bitcast_fusion), calls=%async_computation.5 | async-start | bytes 1048576 | tf_op jit(solution)/shard_map/all_to_all | solution.py:213
  207.7 1.8 fusion.17
  209.5 13.1 %all-to-all-done.4 = bf16[256,8,128]{2,0,1:T(8,128)(2,1)} async-done(((bf16[256,8,128]{2,0,1:T(8,128)(2,1)}), bf16[256,8,128]{2,0,1:T(8,128)(2,1)}, u32[]{:S(2)}, u32[]{:S(2)}) %all-to-all-start.4) | async-done | bytes 524320 | tf_op jit(solution)/shard_map/all_to_all | solution.py:213
  222.6 13.9 %modal_backward.1 = (bf16[2048,128]{1,0:T(8,128)(2,1)}, f32[16,128]{1,0:T(8,128)}, f32[16,128]{1,0:T(8,128)}) custom-call(bf16[2048,128]{1,0:T(8,128)(2,1)} %bitcast.16.x_ref, bf16[2048,128]{1,0:T(8,128)(2,1)} %bitcast.27.g_ref, f32[8,16,128]{2,1,0:T(8,128)} %get-tuple-element.25.entry_ref, f32[16,128]{1,0:T(8,128)} %get-tuple-element.79.decay_ref, ...), custom_call_target="tpu_custom_call" | custom-call | flops 20971520000 | bytes 1572864 | tf_op jit(solution)/shard_map/modal_backward/pallas_call | solution.py:127
  236.5 0.8 multiply_convert_fusion.6
  237.3 1.9 pad_maximum_fusion.4
  239.2 4.2 all-to-all-start.5
  243.5 0.5 all-gather.13.cloned.1.call-update
  244.0 0.2 all-reduce.2.cloned.1.call-start
  244.3 2.2 fusion.15
  246.4 24.7 %all-to-all-done.5 = bf16[8,288,128]{2,1,0:T(8,128)(2,1)} async-done(((bf16[8,288,128]{2,1,0:T(8,128)(2,1)}), bf16[8,288,128]{2,1,0:T(8,128)(2,1)}, u32[]{:S(2)}, u32[]{:S(2)}) %all-to-all-start.5) | async-done | bytes 589856 | tf_op jit(solution)/shard_map/all_to_all | solution.py:226
  271.2 5.2 %all-gather.11.cloned.1.call-done = bf16[2048,512]{1,0:T(8,128)(2,1)} async-done(((bf16[256,512]{1,0:T(8,128)(2,1)}), bf16[2048,512]{1,0:T(8,128)(2,1)}) %all-gather.11.cloned.1.call-update) | async-done | bytes 2097168 | tf_op jit(solution)/shard_map/all_gather | solution.py:201
  276.3 1.1 slice_convert_fusion
  277.5 1.6 copy.42
  279.0 2.4 reshape.72
  281.4 1.7 multiply_convert_fusion.1
  283.3 3.2 fusion.5
  286.7 0.6 copy-done.9
  287.4 0.7 reduce-scatter.2.cloned.1.call-update
  288.1 1.5 pad_maximum_fusion.3
  289.7 1.3 collective-permute-start.1
  291.0 0.2 copy.43
  291.2 1.3 fusion.19
  292.5 0.8 convert_bitcast_fusion
  293.3 0.6 copy.121
  294.0 0.6 copy.120
  294.6 1.1 collective-permute-done.1
  295.7 0.2 pad_maximum_fusion.1
  295.8 3.7 add_convert_fusion
  299.6 26.7 %all-gather.13.cloned.1.call-done = bf16[2048,512]{1,0:T(8,128)(2,1)} async-done(((bf16[256,512]{1,0:T(8,128)(2,1)}), bf16[2048,512]{1,0:T(8,128)(2,1)}) %all-gather.13.cloned.1.call-update) | async-done | bytes 2097168 | tf_op jit(solution)/shard_map/all_gather | solution.py:202
  326.3 3.5 fusion.20
  329.8 1.5 pad_maximum_fusion
  331.3 65.8 %all-reduce.2.cloned.1.call-done = f32[3,7,1024]{2,0,1:T(4,128)} async-done(((f32[3,7,1024]{2,0,1:T(4,128)}), f32[3,7,1024]{2,0,1:T(4,128)}) %all-reduce.2.cloned.1.call-update) | async-done | bytes 86032 | tf_op jit(solution)/shard_map/psum | solution.py:257
  397.0 1.6 copy.46
  398.6 32.9 %reduce-scatter.2.cloned.1.call-done = bf16[256,1024]{1,0:T(8,128)(2,1)} async-done(((bf16[256,4096]{1,0:T(8,128)(2,1)}), bf16[256,1024]{1,0:T(8,128)(2,1)}) %reduce-scatter.2.cloned.1.call-update) | async-done | bytes 524304 | tf_op jit(solution)/shard_map/reduce_scatter | solution.py:212
  (45 shorter events, 0.6 us)
Async XLA Ops:
  7.2 163.2 %all-gather.7.cloned.1.call-start = ((), (), s32[]{:S(2)}) async-start(), calls=%async_computation.7 | async-start | bytes 9437184 | tf_op jit(solution)/shard_map/all_gather | solution.py:191
  8.7 6.6 %collective-permute-start = (bf16[6,3,1024]{2,0,1:T(8,128)(2,1)S(1)}, bf16[6,3,1024]{2,0,1:T(8,128)(2,1)S(1)}, u32[]{:S(2)}, u32[]{:S(2)}) collective-permute-start(bf16[6,3,1024]{2,0,1:T(8,128)(2,1)S(1)} %slice.105), channel_id=1, source_target_pairs={{0,4},{4,8},{8,12},{12,16},{16,20},{20,24},{24,28},{1,5},{5,9},{9,... | collective-permute-start | bytes 110600 | tf_op jit(solution)/shard_map/ppermute | solution.py:12
  23.9 33.0 %all-to-all-start = ((bf16[256,8,128]{2,0,1:T(8,128)(2,1)}), bf16[256,8,128]{2,0,1:T(8,128)(2,1)}, u32[]{:S(2)}, u32[]{:S(2)}) async-start(bf16[256,8,128]{2,0,1:T(8,128)(2,1)} %copy.37), calls=%async_computation | async-start | bytes 1048576 | tf_op jit(solution)/shard_map/all_to_all | solution.py:193
  30.6 163.5 %all-gather.9.cloned.1.call-start = ((), (), s32[]{:S(2)}) async-start(), calls=%async_computation.8 | async-start | bytes 2621440 | tf_op jit(solution)/shard_map/all_gather | solution.py:192
  57.0 13.1 %all-to-all-start.2 = ((bf16[4,64,1024]{2,1,0:T(8,128)(2,1)}), bf16[4,64,1024]{2,1,0:T(8,128)(2,1)}, u32[]{:S(2)}, u32[]{:S(2)}) async-start(bf16[4,64,1024]{2,1,0:T(8,128)(2,1)} %bitcast.130), calls=%async_computation.2 | async-start | bytes 1048576 | tf_op jit(solution)/shard_map/all_to_all | solution.py:197
  70.0 38.9 %all-to-all-start.1 = ((bf16[8,256,128]{2,1,0:T(8,128)(2,1)}), bf16[8,256,128]{2,1,0:T(8,128)(2,1)}, u32[]{:S(2)}, u32[]{:S(2)}) async-start(bf16[8,256,128]{2,1,0:T(8,128)(2,1)} %bitcast.133), calls=%async_computation.1 | async-start | bytes 1048576 | tf_op jit(solution)/shard_map/all_to_all | solution.py:195
  109.0 31.0 %all-to-all-start.3 = ((bf16[64,8,512]{2,0,1:T(8,128)(2,1)}), bf16[64,8,512]{2,0,1:T(8,128)(2,1)}, u32[]{:S(2)}, u32[]{:S(2)}) async-start(bf16[64,8,512]{2,0,1:T(8,128)(2,1)} %copy.40), calls=%async_computation.3 | async-start | bytes 1048576 | tf_op jit(solution)/shard_map/all_to_all | solution.py:198
  113.1 158.0 %all-gather.15.cloned.1.call-start = ((), (), s32[]{:S(2)}) async-start(), calls=%async_computation.13 | async-start | bytes 2621440 | tf_op jit(solution)/shard_map/all_gather | solution.py:203
  202.1 20.5 %all-to-all-start.4 = ((bf16[256,8,128]{2,0,1:T(8,128)(2,1)}), bf16[256,8,128]{2,0,1:T(8,128)(2,1)}, u32[]{:S(2)}, u32[]{:S(2)}) async-start(bf16[256,8,128]{2,0,1:T(8,128)(2,1)} %copy_bitcast_fusion), calls=%async_computation.5 | async-start | bytes 1048576 | tf_op jit(solution)/shard_map/all_to_all | solution.py:213
  207.6 68.7 %all-gather.11.cloned.1.call-start = ((), (), s32[]{:S(2)}) async-start(), calls=%async_computation.10 | async-start | bytes 2359296 | tf_op jit(solution)/shard_map/all_gather | solution.py:201
  239.2 31.9 %all-to-all-start.5 = ((bf16[8,288,128]{2,1,0:T(8,128)(2,1)}), bf16[8,288,128]{2,1,0:T(8,128)(2,1)}, u32[]{:S(2)}, u32[]{:S(2)}) async-start(bf16[8,288,128]{2,1,0:T(8,128)(2,1)} %pad_maximum_fusion.4), calls=%async_computation.6 | async-start | bytes 1179648 | tf_op jit(solution)/shard_map/all_to_all | solution.py:226
  243.4 82.8 %all-gather.13.cloned.1.call-start = ((), (), s32[]{:S(2)}) async-start(), calls=%async_computation.11 | async-start | bytes 2359296 | tf_op jit(solution)/shard_map/all_gather | solution.py:202
  244.0 153.0 %all-reduce.2.cloned.1.call-start = ((), (), s32[]{:S(2)}) async-start(), calls=%async_computation.12 | async-start | bytes 229376 | tf_op jit(solution)/shard_map/psum | solution.py:257
  281.4 1.8 copy-start
  281.4 1.9 copy-start.6
  283.2 3.4 copy-start.2
  283.2 3.4 copy-start.4
  283.2 4.9 %copy-start.1 = (bf16[256,1,1024]{2,0,1:T(8,128)(2,1)S(1)}, bf16[256,1,1024]{2,0,1:T(8,128)(2,1)}, u32[]{:S(2)}) copy-start(bf16[256,1,1024]{2,0,1:T(8,128)(2,1)} %fusion.15) | copy-start | bytes 1572868
  286.6 4.4 %copy-start.7 = (bf16[2048,512]{1,0:T(8,128)(2,1)S(1)}, bf16[2048,512]{1,0:T(8,128)(2,1)}, u32[]{:S(2)}) copy-start(bf16[2048,512]{1,0:T(8,128)(2,1)} %all-gather.15.cloned.1.call-done) | copy-start | bytes 6291460
  286.7 0.6 copy-start.9
  287.4 144.2 %reduce-scatter.2.cloned.1.call-start = ((), (), s32[]{:S(2)}) async-start(), calls=%async_computation.9 | async-start | bytes 2621440 | tf_op jit(solution)/shard_map/reduce_scatter | solution.py:212
  288.1 3.1 copy-start.10
  289.7 6.0 %collective-permute-start.1 = (bf16[6,3,1024]{2,0,1:T(8,128)(2,1)S(1)}, bf16[6,3,1024]{2,0,1:T(8,128)(2,1)S(1)}, u32[]{:S(2)}, u32[]{:S(2)}) collective-permute-start(bf16[6,3,1024]{2,0,1:T(8,128)(2,1)S(1)} %slice.146), channel_id=1, source_target_pairs={{4,0},{8,4},{12,8},{16,12},{20,16},{24,20},{28,24},{5,1},{9,5},{13... | collective-permute-start | bytes 110600 | tf_op jit(solution)/shard_map/ppermute | solution.py:12
  291.2 1.3 copy-start.8
  291.2 4.4 %copy-start.3 = (bf16[256,1,1024]{2,0,1:T(8,128)(2,1)S(1)}, bf16[256,1,1024]{2,0,1:T(8,128)(2,1)}, u32[]{:S(2)}) copy-start(bf16[256,1,1024]{2,0,1:T(8,128)(2,1)} %copy-done.2) | copy-start | bytes 1572868
  291.2 4.4 %copy-start.5 = (bf16[256,1,1024]{2,0,1:T(8,128)(2,1)S(1)}, bf16[256,1,1024]{2,0,1:T(8,128)(2,1)}, u32[]{:S(2)}) copy-start(bf16[256,1,1024]{2,0,1:T(8,128)(2,1)} %copy-done.4) | copy-start | bytes 1572868
Sparse Core Ops, SparseCore 0:
  10.0 160.2 all-gather.6
  171.9 22.1 all-gather.8
  195.6 22.5 all-gather.14
  220.2 56.0 all-gather.10
  278.3 47.9 all-gather.12
  329.5 67.5 all-reduce.1
  400.3 31.1 reduce-scatter.1

commit v2 on v1

--- a/solution.py
+++ b/solution.py
@@ -189,14 +189,19 @@
     local_decay = jnp.exp(-local_rates)
     seq_count = lax.axis_size("seq")
     full_weight = lax.all_gather(w_out, "seq", axis=1, tiled=True)
-    grad_rows = lax.all_gather(cotangent, "tp", axis=1, tiled=True)
+    tp_count = lax.axis_size("tp")
+    copies = jnp.broadcast_to(cotangent, (tp_count,) + cotangent.shape)
+    grad_rows = lax.all_to_all(copies, "tp", split_axis=0, concat_axis=0, tiled=True)
+    grad_rows = grad_rows.transpose(1, 0, 2).reshape(tok_count, -1)
     by_channel = lax.all_to_all(product, "seq", split_axis=1, concat_axis=0, tiled=True)
     conv_channels, entries = modal_output(by_channel, local_decay, local_coeffs)
     convolved = lax.all_to_all(conv_channels, "seq", split_axis=0, concat_axis=1, tiled=True)
     gated = (query_part * convolved).astype(jnp.bfloat16)
     quarter = lax.all_to_all(cotangent, "tp", split_axis=0, concat_axis=1, tiled=True)
     quarter = lax.all_to_all(quarter, "seq", split_axis=1, concat_axis=0, tiled=True)
-    full_weight, gated, quarter = lax.optimization_barrier((full_weight, gated, quarter))
+    full_weight, gated, quarter, grad_rows = lax.optimization_barrier(
+        (full_weight, gated, quarter, grad_rows)
+    )
     half = gated.shape[1] // 2
     gated_first = lax.all_gather(gated[:, :half], "seq", axis=0, tiled=True)
     gated_second = lax.all_gather(gated[:, half:], "seq", axis=0, tiled=True)
@@ -209,7 +214,6 @@
         jnp.bfloat16
     )
     grad_conv, partial_out = lax.optimization_barrier((grad_conv, partial_out))
-    mixed = lax.psum_scatter(partial_out, "tp", scatter_dimension=1, tiled=True)
     grad_channels = lax.all_to_all(grad_conv, "seq", split_axis=1, concat_axis=0, tiled=True)
     back_channels, alpha_rows, beta_rows = modal_grads(
         by_channel, grad_channels, entries, local_decay, local_coeffs
@@ -224,9 +228,17 @@
         axis=1,
     )
     received = lax.all_to_all(sent, "seq", split_axis=0, concat_axis=0, tiled=True)
-    received, gated_first, cot_columns = lax.optimization_barrier(
-        (received, gated_first, cot_columns)
-    )
+    received, gated_first, cot_columns, partial_out = lax.optimization_barrier(
+        (received, gated_first, cot_columns, partial_out)
+    )
+    partials = lax.all_to_all(
+        partial_out.reshape(tok_count, tp_count, -1).transpose(1, 0, 2),
+        "tp",
+        split_axis=0,
+        concat_axis=0,
+        tiled=True,
+    )
+    mixed = jnp.sum(partials.astype(jnp.float32), axis=0).astype(jnp.bfloat16)
     received = received.transpose(1, 0, 2).reshape(tok_count + 2 * mode_count, -1)
     grad_product = received[:tok_count]
     grad_residue = received[tok_count : tok_count + mode_count].astype(jnp.float32)
@@ -254,8 +266,12 @@
             )
         )
     tap_local = jnp.stack(tap_terms, axis=1)
-    grad_taps = lax.psum(tap_local, "seq")
-    tp_count = lax.axis_size("tp")
+    tap_rows = tap_local.shape[0] * tap_local.shape[1]
+    pieces = tap_local.reshape(tap_rows, seq_count, chan_share).transpose(1, 0, 2)
+    pieces = lax.all_to_all(pieces, "seq", split_axis=0, concat_axis=0, tiled=True)
+    tap_sums = jnp.broadcast_to(jnp.sum(pieces, axis=0), (seq_count, tap_rows, chan_share))
+    tap_sums = lax.all_to_all(tap_sums, "seq", split_axis=0, concat_axis=0, tiled=True)
+    grad_taps = tap_sums.transpose(1, 0, 2).reshape(tap_local.shape)
     cot_columns = (
         cot_columns.reshape(tp_count, seq_count, tok_count // tp_count, -1)
         .transpose(1, 0, 2, 3)

time: 440 us -> 333 us (0.76)
  waiting for transfers between devices: 294 us -> 162 us
  starting transfers between devices: 39.1 us -> 54.1 us
  local copies, waits for them, and re-layouts: 20.2 us -> 26.3 us
  other arithmetic: 29.6 us -> 34.3 us
    psum x1 -> x0, waiting for transfers between devices: 65.8 us -> none  [local(): grad_taps = lax.psum(tap_local, 'seq')]
    all_to_all x0 -> x4, waiting for transfers between devices: none -> 42.4 us  [the longest x1 23.7 us: local(): lax.all_to_all(copies, 'tp', split_axis=0, concat_axis=0, tiled=True)]
    reduce_scatter x1 -> x0, waiting for transfers between devices: 32.9 us -> none  [local(): mixed = lax.psum_scatter(partial_out, 'tp', scatter_dimension=1, tiled=True)]
    all_gather x1, waiting for transfers between devices: 30.4 us -> 1.82 us  [local(): full_weight = lax.all_gather(w_out, 'seq', axis=1, tiled=True)]
    all_gather x1, waiting for transfers between devices: 26.7 us -> 4.16 us  [local(): gated_second = lax.all_gather(gated[:, half:], 'seq', axis=0, tiled=True)]
    all_to_all x0 -> x4, starting transfers between devices: none -> 19.7 us  [the longest x1 7.16 us: local(): lax.all_to_all(tap_sums, 'seq', split_axis=0, concat_axis=0, tiled=True)]
    all_gather x1 -> x0, waiting for transfers between devices: 16.4 us -> none  [local(): grad_rows = lax.all_gather(cotangent, 'tp', axis=1, tiled=True)]
  transfers between devices with their start and end apart: 15 -> 16, of which waited for: 14 -> 12; matrix products, arithmetic and copies ran while one was open for 15% -> 22% of each run, Pallas kernels for 5% -> 7%
where the time goes in v2:
time: 333 us; the launch traced here: 331 us
  waiting for transfers between devices  162 us (49%)
  starting transfers between devices  54.1 us (16%)
  other arithmetic  34.3 us (10%)
  local copies, waits for them, and re-layouts  26.3 us (8%)
  Pallas kernels  22 us (7%)
  matrix products  18 us (5%)
  between operations  14.2 us (4%)
    all_to_all x1, waiting for transfers between devices, local(): lax.all_to_all(sent, 'seq', split_axis=0, concat_axis=0, tiled=True)  28.2 us
    all_to_all x1, waiting for transfers between devices, local(): lax.all_to_all(conv_channels, 'seq', split_axis=0, concat_axis=1, tiled=T...  25 us
    all_to_all x1, waiting for transfers between devices, local(): lax.all_to_all(copies, 'tp', split_axis=0, concat_axis=0, tiled=True)  23.7 us
    all_to_all x1, waiting for transfers between devices, local(): lax.all_to_all(product, 'seq', split_axis=1, concat_axis=0, tiled=True)  23.7 us
    all_to_all x1, waiting for transfers between devices, local(): lax.all_to_all(quarter, 'seq', split_axis=1, concat_axis=0, tiled=True)  21.1 us
    pallas_call x1, Pallas kernels, modal_grads(): pl.pallas_call(backward_kernel, grid=(blocks,), in_specs=[rows, rows, pl....  13.9 us
    all_to_all x1, waiting for transfers between devices, local(): lax.all_to_all(grad_conv, 'seq', split_axis=1, concat_axis=0, tiled=True)  12.8 us
    all_to_all x1, waiting for transfers between devices, local(): lax.all_to_all(partial_out.reshape(tok_count, tp_count, -1).transpose(1,...  11.2 us
  transfers between devices with their start and end apart: 16, of which 12 were waited for; matrix products, arithmetic and copies ran while one was open for 22% of the time, Pallas kernels for 7%

profile of v2, /device:TPU:0, one launch (start us, length us, event | category | flops | bytes accessed | tf_op | source)
XLA Modules:
  0.0 331.0 jit_solution(9609370097941034262)
XLA Ops:
  7.2 0.7 all-gather.6.cloned.1.call-update
  7.9 4.2 %all-to-all-start.2 = ((bf16[4,64,1024]{2,1,0:T(8,128)(2,1)}), bf16[4,64,1024]{2,1,0:T(8,128)(2,1)}, u32[]{:S(2)}, u32[]{:S(2)}) async-start(bf16[4,64,1024]{2,1,0:T(8,128)(2,1)} %bitcast.128), calls=%async_computation.2 | async-start | bytes 1048576 | tf_op jit(solution)/shard_map/all_to_all | solution.py:200
  12.1 0.8 slice.105
  12.9 4.8 %collective-permute-start = (bf16[6,3,1024]{2,0,1:T(8,128)(2,1)S(1)}, bf16[6,3,1024]{2,0,1:T(8,128)(2,1)S(1)}, u32[]{:S(2)}, u32[]{:S(2)}) collective-permute-start(bf16[6,3,1024]{2,0,1:T(8,128)(2,1)S(1)} %slice.105), channel_id=1, source_target_pairs={{0,4},{4,8},{8,12},{12,16},{16,20},{20,24},{24,28},{1,5},{5,9},{9,... | collective-permute-start | bytes 110600 | tf_op jit(solution)/shard_map/ppermute | solution.py:12
  17.8 1.5 fusion.17
  19.5 7.2 %multiply_add_fusion = f32[256,3,1024]{2,0,1:T(8,128)S(1)} fusion(bf16[256,3,1024]{2,0,1:T(8,128)(2,1)} %param.6, bf16[6,3,1024]{2,0,1:T(8,128)(2,1)S(1)} %collective-permute-done, f32[3,1024]{1,0:T(4,128)S(1)} %get-tuple-element.68, f32[3,1024]{1,0:T(4,128)S(1)} %get-tuple-element.69, f32[3,1024]{1,0:T(4,128)S(1)} %get-tuple-element.70, ...), kind=kLoop, calls=%fused_computation.21 | loop fusion | flops 29884416 | bytes 4841472 | tf_op jit(solution)/shard_map/add | solution.py:174
  26.9 0.9 copy.49
  27.8 6.7 %all-to-all-start = ((bf16[256,8,128]{2,0,1:T(8,128)(2,1)}), bf16[256,8,128]{2,0,1:T(8,128)(2,1)}, u32[]{:S(2)}, u32[]{:S(2)}) async-start(bf16[256,8,128]{2,0,1:T(8,128)(2,1)} %copy.49), calls=%async_computation | async-start | bytes 1048576 | tf_op jit(solution)/shard_map/all_to_all | solution.py:196
  34.5 1.3 fusion.15
  35.8 2.2 copy.51
  38.1 2.0 all_to_all.91
  40.0 2.0 copy.52
  42.0 23.7 %all-to-all-done = bf16[256,8,128]{2,0,1:T(8,128)(2,1)} async-done(((bf16[256,8,128]{2,0,1:T(8,128)(2,1)}), bf16[256,8,128]{2,0,1:T(8,128)(2,1)}, u32[]{:S(2)}, u32[]{:S(2)}) %all-to-all-start) | async-done | bytes 524320 | tf_op jit(solution)/shard_map/all_to_all | solution.py:196
  65.7 4.2 %all-to-all-start.3 = ((bf16[64,8,512]{2,0,1:T(8,128)(2,1)}), bf16[64,8,512]{2,0,1:T(8,128)(2,1)}, u32[]{:S(2)}, u32[]{:S(2)}) async-start(bf16[64,8,512]{2,0,1:T(8,128)(2,1)} %copy.52), calls=%async_computation.3 | async-start | bytes 1048576 | tf_op jit(solution)/shard_map/all_to_all | solution.py:201
  69.9 8.1 %modal_forward.1 = (bf16[2048,128]{1,0:T(8,128)(2,1)}, f32[8,16,128]{2,1,0:T(8,128)}) custom-call(bf16[2048,128]{1,0:T(8,128)(2,1)} %bitcast.15.x_ref, f32[16,128]{1,0:T(8,128)} %get-tuple-element.65.decay_ref, f32[16,128]{1,0:T(8,128)} %get-tuple-element.64.coeff_ref), custom_call_target="tpu_custom_call" | custom-call | flops 12582912000 | bytes 1048576 | tf_op jit(solution)/shard_map/modal_forward/pallas_call | solution.py:98
  78.0 21.1 %all-to-all-done.3 = bf16[64,8,512]{2,0,1:T(8,128)(2,1)} async-done(((bf16[64,8,512]{2,0,1:T(8,128)(2,1)}), bf16[64,8,512]{2,0,1:T(8,128)(2,1)}, u32[]{:S(2)}, u32[]{:S(2)}) %all-to-all-start.3) | async-done | bytes 524320 | tf_op jit(solution)/shard_map/all_to_all | solution.py:201
  99.1 4.1 %all-to-all-start.1 = ((bf16[8,256,128]{2,1,0:T(8,128)(2,1)}), bf16[8,256,128]{2,1,0:T(8,128)(2,1)}, u32[]{:S(2)}, u32[]{:S(2)}) async-start(bf16[8,256,128]{2,1,0:T(8,128)(2,1)} %bitcast.131), calls=%async_computation.1 | async-start | bytes 1048576 | tf_op jit(solution)/shard_map/all_to_all | solution.py:198
  103.3 2.0 copy.53
  105.3 25.0 %all-to-all-done.1 = bf16[8,256,128]{2,1,0:T(8,128)(2,1)} async-done(((bf16[8,256,128]{2,1,0:T(8,128)(2,1)}), bf16[8,256,128]{2,1,0:T(8,128)(2,1)}, u32[]{:S(2)}, u32[]{:S(2)}) %all-to-all-start.1) | async-done | bytes 524320 | tf_op jit(solution)/shard_map/all_to_all | solution.py:198
  130.4 2.5 broadcast_in_dim.9
  132.9 4.5 %all-to-all-start.4 = ((bf16[4,256,1024]{1,2,0:T(8,128)(2,1)}), bf16[4,256,1024]{1,2,0:T(8,128)(2,1)}, u32[]{:S(2)}, u32[]{:S(2)}) async-start(bf16[4,256,1024]{1,2,0:T(8,128)(2,1)} %broadcast_in_dim.9), calls=%async_computation.4 | async-start | bytes 4194304 | tf_op jit(solution)/shard_map/all_to_all | solution.py:194
  137.4 2.0 multiply_convert_fusion.3
  139.4 23.7 %all-to-all-done.4 = bf16[4,256,1024]{1,2,0:T(8,128)(2,1)} async-done(((bf16[4,256,1024]{1,2,0:T(8,128)(2,1)}), bf16[4,256,1024]{1,2,0:T(8,128)(2,1)}, u32[]{:S(2)}, u32[]{:S(2)}) %all-to-all-start.4) | async-done | bytes 2097184 | tf_op jit(solution)/shard_map/all_to_all | solution.py:194
  163.1 1.8 all-gather.6.cloned.1.call-done
  165.0 7.3 %convolution_convert_fusion = bf16[256,4096]{1,0:T(8,128)(2,1)} fusion(bf16[256,1024]{1,0:T(8,128)(2,1)} %multiply_convert_fusion.3, bf16[1024,4096]{1,0:T(8,128)(2,1)} %all-gather.6.cloned.1.call-done), kind=kOutput, calls=%fused_computation.7 | convolution fusion | flops 2148532224 | bytes 11010048 | tf_op jit(solution)/shard_map/dot_general | solution.py:213
  172.3 4.9 %multiply_convert_fusion.2 = (bf16[256,1024]{1,0:T(8,128)(2,1)S(1)}, bf16[256,1024]{1,0:T(8,128)(2,1)}) fusion(f32[256,3,1024]{2,0,1:T(8,128)S(1)} %multiply_add_fusion, bf16[256,4096]{0,1:T(8,128)(2,1)} %bitcast.25, bf16[1024,4096]{1,0:T(8,128)(2,1)S(1)} %copy-done.10), kind=kOutput, calls=%fused_computation.37 | convolution fusion | flops 2148532224 | bytes 12582912 | tf_op jit(solution)/shard_map/dot_general | solution.py:209
  177.2 0.9 copy_bitcast_fusion
  178.1 4.5 %all-to-all-start.5 = ((bf16[256,8,128]{2,0,1:T(8,128)(2,1)}), bf16[256,8,128]{2,0,1:T(8,128)(2,1)}, u32[]{:S(2)}, u32[]{:S(2)}) async-start(bf16[256,8,128]{2,0,1:T(8,128)(2,1)} %copy_bitcast_fusion), calls=%async_computation.5 | async-start | bytes 1048576 | tf_op jit(solution)/shard_map/all_to_all | solution.py:217
  182.7 1.9 fusion.16
  184.6 12.8 %all-to-all-done.5 = bf16[256,8,128]{2,0,1:T(8,128)(2,1)} async-done(((bf16[256,8,128]{2,0,1:T(8,128)(2,1)}), bf16[256,8,128]{2,0,1:T(8,128)(2,1)}, u32[]{:S(2)}, u32[]{:S(2)}) %all-to-all-start.5) | async-done | bytes 524320 | tf_op jit(solution)/shard_map/all_to_all | solution.py:217
  197.4 13.9 %modal_backward.1 = (bf16[2048,128]{1,0:T(8,128)(2,1)}, f32[16,128]{1,0:T(8,128)}, f32[16,128]{1,0:T(8,128)}) custom-call(bf16[2048,128]{1,0:T(8,128)(2,1)} %bitcast.15.x_ref, bf16[2048,128]{1,0:T(8,128)(2,1)} %bitcast.27.g_ref, f32[8,16,128]{2,1,0:T(8,128)} %get-tuple-element.27.entry_ref, f32[16,128]{1,0:T(8,128)} %get-tuple-element.65.decay_ref, ...), custom_call_target="tpu_custom_call" | custom-call | flops 20971520000 | bytes 1572864 | tf_op jit(solution)/shard_map/modal_backward/pallas_call | solution.py:127
  211.3 0.8 multiply_convert_fusion.6
  212.1 1.9 pad_maximum_fusion.4
  214.0 4.2 %all-to-all-start.6 = ((bf16[8,288,128]{2,1,0:T(8,128)(2,1)}), bf16[8,288,128]{2,1,0:T(8,128)(2,1)}, u32[]{:S(2)}, u32[]{:S(2)}) async-start(bf16[8,288,128]{2,1,0:T(8,128)(2,1)} %pad_maximum_fusion.4), calls=%async_computation.6 | async-start | bytes 1179648 | tf_op jit(solution)/shard_map/all_to_all | solution.py:230
  218.4 0.3 all-gather.10.cloned.1.call-update
  218.8 2.2 fusion.14
  221.0 28.2 %all-to-all-done.6 = bf16[8,288,128]{2,1,0:T(8,128)(2,1)} async-done(((bf16[8,288,128]{2,1,0:T(8,128)(2,1)}), bf16[8,288,128]{2,1,0:T(8,128)(2,1)}, u32[]{:S(2)}, u32[]{:S(2)}) %all-to-all-start.6) | async-done | bytes 589856 | tf_op jit(solution)/shard_map/all_to_all | solution.py:230
  249.1 1.8 all-gather.8.cloned.1.call-done
  250.9 1.1 slice_convert_fusion
  252.0 1.6 copy.56
  253.6 2.4 reshape.88
  256.0 1.8 multiply_convert_fusion.1
  257.9 3.2 fusion.5
  261.4 0.7 copy.58
  262.1 3.6 %all-to-all-start.8 = ((f32[8,21,128]{2,1,0:T(8,128)}), f32[8,21,128]{2,1,0:T(8,128)S(1)}, u32[]{:S(2)}, u32[]{:S(2)}) async-start(f32[8,21,128]{2,1,0:T(8,128)} %copy.58), calls=%async_computation.8 | async-start | bytes 196608 | tf_op jit(solution)/shard_map/all_to_all | solution.py:271
  265.7 1.5 pad_maximum_fusion.3
  267.3 1.3 collective-permute-start.1
  268.8 2.3 fusion.18
  271.1 0.8 convert_bitcast_fusion
  272.0 1.6 copy.137
  273.6 0.6 copy.138
  274.2 0.6 copy.139
  274.9 0.6 broadcast_in_dim.11
  275.5 7.2 %all-to-all-start.9 = ((f32[8,21,128]{2,1,0:T(8,128)}), f32[8,21,128]{2,1,0:T(8,128)S(1)}, u32[]{:S(2)}, u32[]{:S(2)}) async-start(f32[8,21,128]{2,1,0:T(8,128)} %broadcast_in_dim.11), calls=%async_computation.9 | async-start | bytes 196608 | tf_op jit(solution)/shard_map/all_to_all | solution.py:273
  282.7 1.2 pad_maximum_fusion.1
  283.9 7.4 %all-to-all-done.9 = f32[8,21,128]{2,1,0:T(8,128)S(1)} async-done(((f32[8,21,128]{2,1,0:T(8,128)}), f32[8,21,128]{2,1,0:T(8,128)S(1)}, u32[]{:S(2)}, u32[]{:S(2)}) %all-to-all-start.9) | async-done | bytes 86048 | tf_op jit(solution)/shard_map/all_to_all | solution.py:273
  291.4 4.5 %all-to-all-start.7 = ((bf16[4,256,1024]{2,1,0:T(8,128)(2,1)}), bf16[4,256,1024]{2,1,0:T(8,128)(2,1)}, u32[]{:S(2)}, u32[]{:S(2)}) async-start(bf16[4,256,1024]{2,1,0:T(8,128)(2,1)} %bitcast.123), calls=%async_computation.7 | async-start | bytes 4194304 | tf_op jit(solution)/shard_map/all_to_all | solution.py:234
  295.8 4.7 %add_convert_fusion = bf16[256,3,1024]{2,0,1:T(8,128)(2,1)} fusion(bf16[262,3,1024]{2,0,1:T(8,128)(2,1)S(1)} %pad_maximum_fusion.1, f32[3,1024]{1,0:T(4,128)S(1)} %get-tuple-element.68, f32[3,1024]{1,0:T(4,128)S(1)} %get-tuple-element.69, f32[3,1024]{1,0:T(4,128)S(1)} %get-tuple-element.70, f32[3,1024]{1,0:T(4,128)S(1)} %get-tuple-element.71, ...), kind=kLoop, calls=%fused_computation.20 | loop fusion | flops 18087936 | bytes 12668928 | tf_op jit(solution)/shard_map/convert_element_type | solution.py:280
  300.5 4.2 %all-gather.10.cloned.1.call-done = bf16[2048,512]{1,0:T(8,128)(2,1)} async-done(((bf16[256,512]{1,0:T(8,128)(2,1)}), bf16[2048,512]{1,0:T(8,128)(2,1)}) %all-gather.10.cloned.1.call-update) | async-done | bytes 2097168 | tf_op jit(solution)/shard_map/all_gather | solution.py:207
  304.7 3.5 %fusion.19 = f32[512,512]{1,0:T(8,128)S(1)} fusion(bf16[2048,512]{1,0:T(8,128)(2,1)} %all-gather.10.cloned.1.call-done, bf16[2048,512]{1,0:T(8,128)(2,1)} %bitcast.127), kind=kOutput, calls=%fused_computation.66 | convolution fusion | flops 1073741824 | bytes 5242880 | tf_op jit(solution)/shard_map/dot_general | solution.py:284
  308.2 1.5 pad_maximum_fusion
  309.7 0.7 reshape.87
  310.3 11.2 %all-to-all-done.7 = bf16[4,256,1024]{2,1,0:T(8,128)(2,1)} async-done(((bf16[4,256,1024]{2,1,0:T(8,128)(2,1)}), bf16[4,256,1024]{2,1,0:T(8,128)(2,1)}, u32[]{:S(2)}, u32[]{:S(2)}) %all-to-all-start.7) | async-done | bytes 2097184 | tf_op jit(solution)/shard_map/all_to_all | solution.py:234
  321.6 2.9 reduce_sum.21
  (56 shorter events, 1.5 us)
Async XLA Ops:
  7.2 157.8 %all-gather.6.cloned.1.call-start = ((), (), s32[]{:S(2)}) async-start(), calls=%async_computation.10 | async-start | bytes 9437184 | tf_op jit(solution)/shard_map/all_gather | solution.py:191
  7.9 19.9 %all-to-all-start.2 = ((bf16[4,64,1024]{2,1,0:T(8,128)(2,1)}), bf16[4,64,1024]{2,1,0:T(8,128)(2,1)}, u32[]{:S(2)}, u32[]{:S(2)}) async-start(bf16[4,64,1024]{2,1,0:T(8,128)(2,1)} %bitcast.128), calls=%async_computation.2 | async-start | bytes 1048576 | tf_op jit(solution)/shard_map/all_to_all | solution.py:200
  12.9 6.6 %collective-permute-start = (bf16[6,3,1024]{2,0,1:T(8,128)(2,1)S(1)}, bf16[6,3,1024]{2,0,1:T(8,128)(2,1)S(1)}, u32[]{:S(2)}, u32[]{:S(2)}) collective-permute-start(bf16[6,3,1024]{2,0,1:T(8,128)(2,1)S(1)} %slice.105), channel_id=1, source_target_pairs={{0,4},{4,8},{8,12},{12,16},{16,20},{20,24},{24,28},{1,5},{5,9},{9,... | collective-permute-start | bytes 110600 | tf_op jit(solution)/shard_map/ppermute | solution.py:12
  27.8 37.9 %all-to-all-start = ((bf16[256,8,128]{2,0,1:T(8,128)(2,1)}), bf16[256,8,128]{2,0,1:T(8,128)(2,1)}, u32[]{:S(2)}, u32[]{:S(2)}) async-start(bf16[256,8,128]{2,0,1:T(8,128)(2,1)} %copy.49), calls=%async_computation | async-start | bytes 1048576 | tf_op jit(solution)/shard_map/all_to_all | solution.py:196
  65.7 33.4 %all-to-all-start.3 = ((bf16[64,8,512]{2,0,1:T(8,128)(2,1)}), bf16[64,8,512]{2,0,1:T(8,128)(2,1)}, u32[]{:S(2)}, u32[]{:S(2)}) async-start(bf16[64,8,512]{2,0,1:T(8,128)(2,1)} %copy.52), calls=%async_computation.3 | async-start | bytes 1048576 | tf_op jit(solution)/shard_map/all_to_all | solution.py:201
  99.1 31.2 %all-to-all-start.1 = ((bf16[8,256,128]{2,1,0:T(8,128)(2,1)}), bf16[8,256,128]{2,1,0:T(8,128)(2,1)}, u32[]{:S(2)}, u32[]{:S(2)}) async-start(bf16[8,256,128]{2,1,0:T(8,128)(2,1)} %bitcast.131), calls=%async_computation.1 | async-start | bytes 1048576 | tf_op jit(solution)/shard_map/all_to_all | solution.py:198
  132.9 30.2 %all-to-all-start.4 = ((bf16[4,256,1024]{1,2,0:T(8,128)(2,1)}), bf16[4,256,1024]{1,2,0:T(8,128)(2,1)}, u32[]{:S(2)}, u32[]{:S(2)}) async-start(bf16[4,256,1024]{1,2,0:T(8,128)(2,1)} %broadcast_in_dim.9), calls=%async_computation.4 | async-start | bytes 4194304 | tf_op jit(solution)/shard_map/all_to_all | solution.py:194
  137.3 111.8 %all-gather.12.cloned.1.call-start = ((), (), s32[]{:S(2)}) async-start(), calls=%async_computation.13 | async-start | bytes 2621440 | tf_op jit(solution)/shard_map/all_gather | solution.py:208
  164.9 7.4 %copy-start.10 = (bf16[1024,4096]{1,0:T(8,128)(2,1)S(1)}, bf16[1024,4096]{1,0:T(8,128)(2,1)}, u32[]{:S(2)}) copy-start(bf16[1024,4096]{1,0:T(8,128)(2,1)} %all-gather.6.cloned.1.call-done) | copy-start | bytes 25165828
  178.1 19.3 %all-to-all-start.5 = ((bf16[256,8,128]{2,0,1:T(8,128)(2,1)}), bf16[256,8,128]{2,0,1:T(8,128)(2,1)}, u32[]{:S(2)}, u32[]{:S(2)}) async-start(bf16[256,8,128]{2,0,1:T(8,128)(2,1)} %copy_bitcast_fusion), calls=%async_computation.5 | async-start | bytes 1048576 | tf_op jit(solution)/shard_map/all_to_all | solution.py:217
  182.6 68.3 %all-gather.8.cloned.1.call-start = ((), (), s32[]{:S(2)}) async-start(), calls=%async_computation.11 | async-start | bytes 2359296 | tf_op jit(solution)/shard_map/all_gather | solution.py:206
  214.0 35.1 %all-to-all-start.6 = ((bf16[8,288,128]{2,1,0:T(8,128)(2,1)}), bf16[8,288,128]{2,1,0:T(8,128)(2,1)}, u32[]{:S(2)}, u32[]{:S(2)}) async-start(bf16[8,288,128]{2,1,0:T(8,128)(2,1)} %pad_maximum_fusion.4), calls=%async_computation.6 | async-start | bytes 1179648 | tf_op jit(solution)/shard_map/all_to_all | solution.py:230
  218.2 86.5 %all-gather.10.cloned.1.call-start = ((), (), s32[]{:S(2)}) async-start(), calls=%async_computation.12 | async-start | bytes 2359296 | tf_op jit(solution)/shard_map/all_gather | solution.py:207
  256.0 1.8 copy-start
  256.0 1.9 copy-start.5
  257.7 3.4 %copy-start.2 = (bf16[256,1,1024]{2,0,1:T(8,128)(2,1)}, bf16[256,1,1024]{2,0,1:T(8,128)(2,1)S(1)}, u32[]{:S(2)}) copy-start(bf16[256,1,1024]{2,0,1:T(8,128)(2,1)S(1)} %get-tuple-element.45) | copy-start | bytes 1572868
  257.7 3.4 %copy-start.4 = (bf16[256,1,1024]{2,0,1:T(8,128)(2,1)}, bf16[256,1,1024]{2,0,1:T(8,128)(2,1)S(1)}, u32[]{:S(2)}) copy-start(bf16[256,1,1024]{2,0,1:T(8,128)(2,1)S(1)} %get-tuple-element.46) | copy-start | bytes 1572868
  257.8 7.9 %copy-start.1 = (bf16[256,1,1024]{2,0,1:T(8,128)(2,1)S(1)}, bf16[256,1,1024]{2,0,1:T(8,128)(2,1)}, u32[]{:S(2)}) copy-start(bf16[256,1,1024]{2,0,1:T(8,128)(2,1)} %fusion.14) | copy-start | bytes 1572868
  257.9 10.7 %copy-start.7 = (bf16[2048,512]{1,0:T(8,128)(2,1)S(1)}, bf16[2048,512]{1,0:T(8,128)(2,1)}, u32[]{:S(2)}) copy-start(bf16[2048,512]{1,0:T(8,128)(2,1)} %all-gather.12.cloned.1.call-done) | copy-start | bytes 6291460
  262.1 12.8 %all-to-all-start.8 = ((f32[8,21,128]{2,1,0:T(8,128)}), f32[8,21,128]{2,1,0:T(8,128)S(1)}, u32[]{:S(2)}, u32[]{:S(2)}) async-start(f32[8,21,128]{2,1,0:T(8,128)} %copy.58), calls=%async_computation.8 | async-start | bytes 196608 | tf_op jit(solution)/shard_map/all_to_all | solution.py:271
  265.7 3.1 copy-start.11
  267.3 15.4 %collective-permute-start.1 = (bf16[6,3,1024]{2,0,1:T(8,128)(2,1)S(1)}, bf16[6,3,1024]{2,0,1:T(8,128)(2,1)S(1)}, u32[]{:S(2)}, u32[]{:S(2)}) collective-permute-start(bf16[6,3,1024]{2,0,1:T(8,128)(2,1)S(1)} %slice.146), channel_id=1, source_target_pairs={{4,0},{8,4},{12,8},{16,12},{20,16},{24,20},{28,24},{5,1},{9,5},{13... | collective-permute-start | bytes 110600 | tf_op jit(solution)/shard_map/ppermute | solution.py:12
  268.8 2.3 copy-start.8
  268.8 3.2 copy-start.6
  271.1 11.6 %copy-start.3 = (bf16[256,1,1024]{2,0,1:T(8,128)(2,1)S(1)}, bf16[256,1,1024]{2,0,1:T(8,128)(2,1)}, u32[]{:S(2)}) copy-start(bf16[256,1,1024]{2,0,1:T(8,128)(2,1)} %copy-done.2) | copy-start | bytes 1572868
  275.5 15.8 %all-to-all-start.9 = ((f32[8,21,128]{2,1,0:T(8,128)}), f32[8,21,128]{2,1,0:T(8,128)S(1)}, u32[]{:S(2)}, u32[]{:S(2)}) async-start(f32[8,21,128]{2,1,0:T(8,128)} %broadcast_in_dim.11), calls=%async_computation.9 | async-start | bytes 196608 | tf_op jit(solution)/shard_map/all_to_all | solution.py:273
  291.4 30.2 %all-to-all-start.7 = ((bf16[4,256,1024]{2,1,0:T(8,128)(2,1)}), bf16[4,256,1024]{2,1,0:T(8,128)(2,1)}, u32[]{:S(2)}, u32[]{:S(2)}) async-start(bf16[4,256,1024]{2,1,0:T(8,128)(2,1)} %bitcast.123), calls=%async_computation.7 | async-start | bytes 4194304 | tf_op jit(solution)/shard_map/all_to_all | solution.py:234
  300.5 7.7 %copy-start.9 = (f32[512,512]{1,0:T(8,128)S(1)}, f32[512,512]{1,0:T(8,128)}, u32[]{:S(2)}) copy-start(f32[512,512]{1,0:T(8,128)} %fusion.18) | copy-start | bytes 3145732
Sparse Core Ops, SparseCore 0:
  10.0 154.8 all-gather.5
  166.5 22.3 all-gather.11
  191.0 59.7 all-gather.7
  252.9 51.7 all-gather.9

commit v3 on v2

--- a/solution.py
+++ b/solution.py
@@ -213,7 +213,6 @@
     partial_out = jnp.dot(gated, full_weight, preferred_element_type=jnp.float32).astype(
         jnp.bfloat16
     )
-    grad_conv, partial_out = lax.optimization_barrier((grad_conv, partial_out))
     grad_channels = lax.all_to_all(grad_conv, "seq", split_axis=1, concat_axis=0, tiled=True)
     back_channels, alpha_rows, beta_rows = modal_grads(
         by_channel, grad_channels, entries, local_decay, local_coeffs
@@ -238,7 +237,6 @@
         concat_axis=0,
         tiled=True,
     )
-    mixed = jnp.sum(partials.astype(jnp.float32), axis=0).astype(jnp.bfloat16)
     received = received.transpose(1, 0, 2).reshape(tok_count + 2 * mode_count, -1)
     grad_product = received[:tok_count]
     grad_residue = received[tok_count : tok_count + mode_count].astype(jnp.float32)
@@ -268,6 +266,8 @@
     tap_local = jnp.stack(tap_terms, axis=1)
     tap_rows = tap_local.shape[0] * tap_local.shape[1]
     pieces = tap_local.reshape(tap_rows, seq_count, chan_share).transpose(1, 0, 2)
+    pieces, partials = lax.optimization_barrier((pieces, partials))
+    mixed = jnp.sum(partials.astype(jnp.float32), axis=0).astype(jnp.bfloat16)
     pieces = lax.all_to_all(pieces, "seq", split_axis=0, concat_axis=0, tiled=True)
     tap_sums = jnp.broadcast_to(jnp.sum(pieces, axis=0), (seq_count, tap_rows, chan_share))
     tap_sums = lax.all_to_all(tap_sums, "seq", split_axis=0, concat_axis=0, tiled=True)

time: 333 us -> 330 us (level)
  blocking collectives: 0 us -> 19.3 us
  waiting for transfers between devices: 162 us -> 146 us
  starting transfers between devices: 54.1 us -> 48.2 us
    all_to_all x0 -> x1, blocking collectives: none -> 19.3 us  [local(): lax.all_to_all(grad_conv, 'seq', split_axis=1, concat_axis=0, tiled=True)]
    all_gather x1, waiting for transfers between devices: 4.16 us -> 22.6 us  [local(): gated_second = lax.all_gather(gated[:, half:], 'seq', axis=0, tiled=True)]
    all_to_all x1 -> x0, waiting for transfers between devices: 12.8 us -> none  [local(): lax.all_to_all(grad_conv, 'seq', split_axis=1, concat_axis=0, tiled=True)]
    all_to_all x1, waiting for transfers between devices: 11.2 us -> 0.01 us  [local(): lax.all_to_all(partial_out.reshape(tok_count, tp_count, -1).transpose(1,...]
    all_to_all x1, waiting for transfers between devices: 28.2 us -> 19 us  [local(): lax.all_to_all(sent, 'seq', split_axis=0, concat_axis=0, tiled=True)]
    all_to_all x1, waiting for transfers between devices: 7.42 us -> 2.65 us  [local(): lax.all_to_all(tap_sums, 'seq', split_axis=0, concat_axis=0, tiled=True)]
    all_to_all x1, waiting for transfers between devices: 21.1 us -> 16.6 us  [local(): lax.all_to_all(quarter, 'seq', split_axis=1, concat_axis=0, tiled=True)]
    all_to_all x1 -> x0, starting transfers between devices: 4.53 us -> none  [local(): lax.all_to_all(grad_conv, 'seq', split_axis=1, concat_axis=0, tiled=True)]
  transfers between devices with their start and end apart: 16 -> 15, of which waited for: 12 -> 11; matrix products, arithmetic and copies ran while one was open for 22% -> 23% of each run, Pallas kernels for 7% -> 7%
where the time goes in v3:
time: 330 us; the launch traced here: 328 us
  waiting for transfers between devices  146 us (44%)
  starting transfers between devices  48.2 us (15%)
  other arithmetic  32.2 us (10%)
  local copies, waits for them, and re-layouts  26.7 us (8%)
  Pallas kernels  22 us (7%)
  matrix products  19.5 us (6%)
  blocking collectives  19.3 us (6%)
  between operations  14.2 us (4%)
    all_to_all x1, waiting for transfers between devices, local(): lax.all_to_all(conv_channels, 'seq', split_axis=0, concat_axis=1, tiled=T...  25.4 us
    all_to_all x1, waiting for transfers between devices, local(): lax.all_to_all(copies, 'tp', split_axis=0, concat_axis=0, tiled=True)  23.7 us
    all_to_all x1, waiting for transfers between devices, local(): lax.all_to_all(product, 'seq', split_axis=1, concat_axis=0, tiled=True)  23.7 us
    all_gather x1, waiting for transfers between devices, local(): gated_second = lax.all_gather(gated[:, half:], 'seq', axis=0, tiled=True)  22.6 us
    all_to_all x1, blocking collectives, local(): lax.all_to_all(grad_conv, 'seq', split_axis=1, concat_axis=0, tiled=True)  19.3 us
    all_to_all x1, waiting for transfers between devices, local(): lax.all_to_all(sent, 'seq', split_axis=0, concat_axis=0, tiled=True)  19 us
    all_to_all x1, waiting for transfers between devices, local(): lax.all_to_all(quarter, 'seq', split_axis=1, concat_axis=0, tiled=True)  16.6 us
    pallas_call x1, Pallas kernels, modal_grads(): pl.pallas_call(backward_kernel, grid=(blocks,), in_specs=[rows, rows, pl....  13.9 us
  transfers between devices with their start and end apart: 15, of which 11 were waited for; matrix products, arithmetic and copies ran while one was open for 23% of the time, Pallas kernels for 7%

profile of v3, /device:TPU:0, one launch (start us, length us, event | category | flops | bytes accessed | tf_op | source)
XLA Modules:
  0.0 328.0 jit_solution(11935322381487563835)
XLA Ops:
  7.2 0.7 all-gather.6.cloned.1.call-update
  7.9 4.2 %all-to-all-start.2 = ((bf16[4,64,1024]{2,1,0:T(8,128)(2,1)}), bf16[4,64,1024]{2,1,0:T(8,128)(2,1)}, u32[]{:S(2)}, u32[]{:S(2)}) async-start(bf16[4,64,1024]{2,1,0:T(8,128)(2,1)} %bitcast.131), calls=%async_computation.2 | async-start | bytes 1048576 | tf_op jit(solution)/shard_map/all_to_all | solution.py:200
  12.1 0.8 slice.105
  12.9 4.8 %collective-permute-start = (bf16[6,3,1024]{2,0,1:T(8,128)(2,1)S(1)}, bf16[6,3,1024]{2,0,1:T(8,128)(2,1)S(1)}, u32[]{:S(2)}, u32[]{:S(2)}) collective-permute-start(bf16[6,3,1024]{2,0,1:T(8,128)(2,1)S(1)} %slice.105), channel_id=1, source_target_pairs={{0,4},{4,8},{8,12},{12,16},{16,20},{20,24},{24,28},{1,5},{5,9},{9,... | collective-permute-start | bytes 110600 | tf_op jit(solution)/shard_map/ppermute | solution.py:12
  17.8 1.5 fusion.18
  19.5 7.4 %multiply_add_fusion = f32[256,3,1024]{2,0,1:T(8,128)S(1)} fusion(bf16[256,3,1024]{2,0,1:T(8,128)(2,1)} %param.6, bf16[6,3,1024]{2,0,1:T(8,128)(2,1)S(1)} %collective-permute-done, f32[3,1024]{1,0:T(4,128)S(1)} %get-tuple-element.66, f32[3,1024]{1,0:T(4,128)S(1)} %get-tuple-element.67, f32[3,1024]{1,0:T(4,128)S(1)} %get-tuple-element.68, ...), kind=kLoop, calls=%fused_computation.21 | loop fusion | flops 29884416 | bytes 4841472 | tf_op jit(solution)/shard_map/add | solution.py:174
  27.0 0.2 fusion.13
  27.2 0.9 copy.49
  28.1 6.7 %all-to-all-start = ((bf16[256,8,128]{2,0,1:T(8,128)(2,1)}), bf16[256,8,128]{2,0,1:T(8,128)(2,1)}, u32[]{:S(2)}, u32[]{:S(2)}) async-start(bf16[256,8,128]{2,0,1:T(8,128)(2,1)} %copy.49), calls=%async_computation | async-start | bytes 1048576 | tf_op jit(solution)/shard_map/all_to_all | solution.py:196
  34.8 1.3 fusion.16
  36.1 2.2 copy.51
  38.4 2.0 all_to_all.91
  40.3 2.0 copy.52
  42.3 23.7 %all-to-all-done = bf16[256,8,128]{2,0,1:T(8,128)(2,1)} async-done(((bf16[256,8,128]{2,0,1:T(8,128)(2,1)}), bf16[256,8,128]{2,0,1:T(8,128)(2,1)}, u32[]{:S(2)}, u32[]{:S(2)}) %all-to-all-start) | async-done | bytes 524320 | tf_op jit(solution)/shard_map/all_to_all | solution.py:196
  66.1 4.2 %all-to-all-start.3 = ((bf16[64,8,512]{2,0,1:T(8,128)(2,1)}), bf16[64,8,512]{2,0,1:T(8,128)(2,1)}, u32[]{:S(2)}, u32[]{:S(2)}) async-start(bf16[64,8,512]{2,0,1:T(8,128)(2,1)} %copy.52), calls=%async_computation.3 | async-start | bytes 1048576 | tf_op jit(solution)/shard_map/all_to_all | solution.py:201
  70.2 8.1 %modal_forward.1 = (bf16[2048,128]{1,0:T(8,128)(2,1)}, f32[8,16,128]{2,1,0:T(8,128)}) custom-call(bf16[2048,128]{1,0:T(8,128)(2,1)} %bitcast.16.x_ref, f32[16,128]{1,0:T(8,128)} %get-tuple-element.65.decay_ref, f32[16,128]{1,0:T(8,128)} %get-tuple-element.64.coeff_ref), custom_call_target="tpu_custom_call" | custom-call | flops 12582912000 | bytes 1048576 | tf_op jit(solution)/shard_map/modal_forward/pallas_call | solution.py:98
  78.3 16.6 %all-to-all-done.3 = bf16[64,8,512]{2,0,1:T(8,128)(2,1)} async-done(((bf16[64,8,512]{2,0,1:T(8,128)(2,1)}), bf16[64,8,512]{2,0,1:T(8,128)(2,1)}, u32[]{:S(2)}, u32[]{:S(2)}) %all-to-all-start.3) | async-done | bytes 524320 | tf_op jit(solution)/shard_map/all_to_all | solution.py:201
  94.9 6.7 %all-to-all-start.1 = ((bf16[8,256,128]{2,1,0:T(8,128)(2,1)}), bf16[8,256,128]{2,1,0:T(8,128)(2,1)}, u32[]{:S(2)}, u32[]{:S(2)}) async-start(bf16[8,256,128]{2,1,0:T(8,128)(2,1)} %bitcast.134), calls=%async_computation.1 | async-start | bytes 1048576 | tf_op jit(solution)/shard_map/all_to_all | solution.py:198
  101.6 2.0 copy.53
  103.7 25.4 %all-to-all-done.1 = bf16[8,256,128]{2,1,0:T(8,128)(2,1)} async-done(((bf16[8,256,128]{2,1,0:T(8,128)(2,1)}), bf16[8,256,128]{2,1,0:T(8,128)(2,1)}, u32[]{:S(2)}, u32[]{:S(2)}) %all-to-all-start.1) | async-done | bytes 524320 | tf_op jit(solution)/shard_map/all_to_all | solution.py:198
  129.1 2.5 broadcast_in_dim.9
  131.6 4.5 %all-to-all-start.4 = ((bf16[4,256,1024]{1,2,0:T(8,128)(2,1)}), bf16[4,256,1024]{1,2,0:T(8,128)(2,1)}, u32[]{:S(2)}, u32[]{:S(2)}) async-start(bf16[4,256,1024]{1,2,0:T(8,128)(2,1)} %broadcast_in_dim.9), calls=%async_computation.4 | async-start | bytes 4194304 | tf_op jit(solution)/shard_map/all_to_all | solution.py:194
  136.1 2.0 multiply_convert_fusion.3
  138.1 23.7 %all-to-all-done.4 = bf16[4,256,1024]{1,2,0:T(8,128)(2,1)} async-done(((bf16[4,256,1024]{1,2,0:T(8,128)(2,1)}), bf16[4,256,1024]{1,2,0:T(8,128)(2,1)}, u32[]{:S(2)}, u32[]{:S(2)}) %all-to-all-start.4) | async-done | bytes 2097184 | tf_op jit(solution)/shard_map/all_to_all | solution.py:194
  161.8 3.8 %all-gather.6.cloned.1.call-done = bf16[1024,4096]{1,0:T(8,128)(2,1)} async-done(((bf16[1024,512]{1,0:T(8,128)(2,1)}), bf16[1024,4096]{1,0:T(8,128)(2,1)}) %all-gather.6.cloned.1.call-update) | async-done | bytes 8388624 | tf_op jit(solution)/shard_map/all_gather | solution.py:191
  165.7 1.9 fusion.17
  167.6 7.2 %convolution_convert_fusion.1 = bf16[256,1024]{1,0:T(8,128)(2,1)} fusion(bf16[256,4096]{0,1:T(8,128)(2,1)} %bitcast.24, bf16[1024,4096]{1,0:T(8,128)(2,1)} %all-gather.6.cloned.1.call-done), kind=kOutput, calls=%fused_computation.33 | convolution fusion | flops 2147745792 | bytes 11010048 | tf_op jit(solution)/shard_map/dot_general | solution.py:209
  174.8 1.2 copy_bitcast_fusion
  176.0 19.3 %all_to_all.114 = bf16[256,8,128]{2,0,1:T(8,128)(2,1)} all-to-all(bf16[256,8,128]{2,0,1:T(8,128)(2,1)S(1)} %copy_bitcast_fusion), channel_id=1, replica_groups=mesh['seq'=8,'tp'=4] {'seq'}, dimensions={1} | all-to-all | bytes 1048576 | tf_op jit(solution)/shard_map/all_to_all | solution.py:216
  195.3 13.9 %modal_backward.1 = (bf16[2048,128]{1,0:T(8,128)(2,1)}, f32[16,128]{1,0:T(8,128)}, f32[16,128]{1,0:T(8,128)}) custom-call(bf16[2048,128]{1,0:T(8,128)(2,1)} %bitcast.16.x_ref, bf16[2048,128]{1,0:T(8,128)(2,1)} %bitcast.135, f32[8,16,128]{2,1,0:T(8,128)} %get-tuple-element.25.entry_ref, f32[16,128]{1,0:T(8,128)} %get-tuple-element.65.decay_ref, ...), custom_call_target="tpu_custom_call" | custom-call | flops 20971520000 | bytes 1572864 | tf_op jit(solution)/shard_map/modal_backward/pallas_call | solution.py:127
  209.2 0.8 multiply_convert_fusion.6
  210.0 1.9 pad_maximum_fusion.4
  211.9 4.2 %all-to-all-start.6 = ((bf16[8,288,128]{2,1,0:T(8,128)(2,1)}), bf16[8,288,128]{2,1,0:T(8,128)(2,1)}, u32[]{:S(2)}, u32[]{:S(2)}) async-start(bf16[8,288,128]{2,1,0:T(8,128)(2,1)} %pad_maximum_fusion.4), calls=%async_computation.6 | async-start | bytes 1179648 | tf_op jit(solution)/shard_map/all_to_all | solution.py:229
  216.2 0.5 all-gather.10.cloned.1.call-update
  216.7 7.5 %convolution_convert_fusion = bf16[256,4096]{1,0:T(8,128)(2,1)} fusion(bf16[256,1024]{1,0:T(8,128)(2,1)} %multiply_convert_fusion.3, bf16[1024,4096]{1,0:T(8,128)(2,1)} %all-gather.6.cloned.1.call-done), kind=kOutput, calls=%fused_computation.7 | convolution fusion | flops 2148532224 | bytes 11010048 | tf_op jit(solution)/shard_map/dot_general | solution.py:213
  224.2 2.0 fusion.15
  226.2 19.0 %all-to-all-done.6 = bf16[8,288,128]{2,1,0:T(8,128)(2,1)} async-done(((bf16[8,288,128]{2,1,0:T(8,128)(2,1)}), bf16[8,288,128]{2,1,0:T(8,128)(2,1)}, u32[]{:S(2)}, u32[]{:S(2)}) %all-to-all-start.6) | async-done | bytes 589856 | tf_op jit(solution)/shard_map/all_to_all | solution.py:229
  245.2 3.3 %all-gather.8.cloned.1.call-done = bf16[2048,512]{1,0:T(8,128)(2,1)} async-done(((bf16[256,512]{1,0:T(8,128)(2,1)}), bf16[2048,512]{1,0:T(8,128)(2,1)}) %all-gather.8.cloned.1.call-update) | async-done | bytes 2097168 | tf_op jit(solution)/shard_map/all_gather | solution.py:206
  248.5 3.1 copy.137
  251.7 4.6 %all-to-all-start.7 = ((bf16[4,256,1024]{2,1,0:T(8,128)(2,1)}), bf16[4,256,1024]{2,1,0:T(8,128)(2,1)}, u32[]{:S(2)}, u32[]{:S(2)}) async-start(bf16[4,256,1024]{2,1,0:T(8,128)(2,1)} %bitcast.126), calls=%async_computation.7 | async-start | bytes 4194304 | tf_op jit(solution)/shard_map/all_to_all | solution.py:233
  256.3 1.1 slice_convert_fusion
  257.5 1.6 copy.55
  259.0 2.4 reshape.88
  261.4 1.7 multiply_convert_fusion.1
  263.2 0.2 pad_maximum_fusion.3
  263.4 1.4 collective-permute-start.1
  264.8 0.2 copy.57
  265.1 3.3 fusion.5
  268.4 1.3 fusion.19
  269.7 0.8 convert_bitcast_fusion
  270.5 0.6 copy.138
  271.1 0.6 copy.139
  272.3 3.7 %add_convert_fusion = bf16[256,3,1024]{2,0,1:T(8,128)(2,1)} fusion(bf16[262,3,1024]{2,0,1:T(8,128)(2,1)S(1)} %pad_maximum_fusion.1, f32[3,1024]{1,0:T(4,128)S(1)} %get-tuple-element.66, f32[3,1024]{1,0:T(4,128)S(1)} %get-tuple-element.67, f32[3,1024]{1,0:T(4,128)S(1)} %get-tuple-element.68, f32[3,1024]{1,0:T(4,128)S(1)} %get-tuple-element.69, ...), kind=kLoop, calls=%fused_computation.20 | loop fusion | flops 18087936 | bytes 12668928 | tf_op jit(solution)/shard_map/convert_element_type | solution.py:280
  276.0 22.6 %all-gather.10.cloned.1.call-done = bf16[2048,512]{1,0:T(8,128)(2,1)} async-done(((bf16[256,512]{1,0:T(8,128)(2,1)}), bf16[2048,512]{1,0:T(8,128)(2,1)}) %all-gather.10.cloned.1.call-update) | async-done | bytes 2097168 | tf_op jit(solution)/shard_map/all_gather | solution.py:207
  298.6 0.7 copy.58
  299.3 3.4 %all-to-all-start.8 = ((f32[8,21,128]{2,1,0:T(8,128)}), f32[8,21,128]{2,1,0:T(8,128)S(1)}, u32[]{:S(2)}, u32[]{:S(2)}) async-start(f32[8,21,128]{2,1,0:T(8,128)} %copy.58), calls=%async_computation.8 | async-start | bytes 196608 | tf_op jit(solution)/shard_map/all_to_all | solution.py:271
  302.7 3.5 %fusion.20 = f32[512,512]{1,0:T(8,128)S(1)} fusion(bf16[2048,512]{1,0:T(8,128)(2,1)} %all-gather.10.cloned.1.call-done, bf16[2048,512]{1,0:T(8,128)(2,1)} %bitcast.129), kind=kOutput, calls=%fused_computation.67 | convolution fusion | flops 1073741824 | bytes 5242880 | tf_op jit(solution)/shard_map/dot_general | solution.py:284
  306.2 3.6 %all-to-all-done.8 = f32[8,21,128]{2,1,0:T(8,128)S(1)} async-done(((f32[8,21,128]{2,1,0:T(8,128)}), f32[8,21,128]{2,1,0:T(8,128)S(1)}, u32[]{:S(2)}, u32[]{:S(2)}) %all-to-all-start.8) | async-done | bytes 86048 | tf_op jit(solution)/shard_map/all_to_all | solution.py:271
  309.7 0.6 broadcast_in_dim.11
  310.4 3.4 %all-to-all-start.9 = ((f32[8,21,128]{2,1,0:T(8,128)}), f32[8,21,128]{2,1,0:T(8,128)S(1)}, u32[]{:S(2)}, u32[]{:S(2)}) async-start(f32[8,21,128]{2,1,0:T(8,128)} %broadcast_in_dim.11), calls=%async_computation.9 | async-start | bytes 196608 | tf_op jit(solution)/shard_map/all_to_all | solution.py:273
  313.8 1.5 pad_maximum_fusion
  315.3 2.9 reduce_sum.21
  318.2 2.6 all-to-all-done.9
  320.8 0.7 reshape.87
  (53 shorter events, 1.0 us)
Async XLA Ops:
  7.2 158.5 %all-gather.6.cloned.1.call-start = ((), (), s32[]{:S(2)}) async-start(), calls=%async_computation.10 | async-start | bytes 9437184 | tf_op jit(solution)/shard_map/all_gather | solution.py:191
  7.9 20.2 %all-to-all-start.2 = ((bf16[4,64,1024]{2,1,0:T(8,128)(2,1)}), bf16[4,64,1024]{2,1,0:T(8,128)(2,1)}, u32[]{:S(2)}, u32[]{:S(2)}) async-start(bf16[4,64,1024]{2,1,0:T(8,128)(2,1)} %bitcast.131), calls=%async_computation.2 | async-start | bytes 1048576 | tf_op jit(solution)/shard_map/all_to_all | solution.py:200
  12.9 6.6 %collective-permute-start = (bf16[6,3,1024]{2,0,1:T(8,128)(2,1)S(1)}, bf16[6,3,1024]{2,0,1:T(8,128)(2,1)S(1)}, u32[]{:S(2)}, u32[]{:S(2)}) collective-permute-start(bf16[6,3,1024]{2,0,1:T(8,128)(2,1)S(1)} %slice.105), channel_id=1, source_target_pairs={{0,4},{4,8},{8,12},{12,16},{16,20},{20,24},{24,28},{1,5},{5,9},{9,... | collective-permute-start | bytes 110600 | tf_op jit(solution)/shard_map/ppermute | solution.py:12
  28.1 37.9 %all-to-all-start = ((bf16[256,8,128]{2,0,1:T(8,128)(2,1)}), bf16[256,8,128]{2,0,1:T(8,128)(2,1)}, u32[]{:S(2)}, u32[]{:S(2)}) async-start(bf16[256,8,128]{2,0,1:T(8,128)(2,1)} %copy.49), calls=%async_computation | async-start | bytes 1048576 | tf_op jit(solution)/shard_map/all_to_all | solution.py:196
  66.1 28.8 %all-to-all-start.3 = ((bf16[64,8,512]{2,0,1:T(8,128)(2,1)}), bf16[64,8,512]{2,0,1:T(8,128)(2,1)}, u32[]{:S(2)}, u32[]{:S(2)}) async-start(bf16[64,8,512]{2,0,1:T(8,128)(2,1)} %copy.52), calls=%async_computation.3 | async-start | bytes 1048576 | tf_op jit(solution)/shard_map/all_to_all | solution.py:201
  94.9 34.2 %all-to-all-start.1 = ((bf16[8,256,128]{2,1,0:T(8,128)(2,1)}), bf16[8,256,128]{2,1,0:T(8,128)(2,1)}, u32[]{:S(2)}, u32[]{:S(2)}) async-start(bf16[8,256,128]{2,1,0:T(8,128)(2,1)} %bitcast.134), calls=%async_computation.1 | async-start | bytes 1048576 | tf_op jit(solution)/shard_map/all_to_all | solution.py:198
  131.6 30.2 %all-to-all-start.4 = ((bf16[4,256,1024]{1,2,0:T(8,128)(2,1)}), bf16[4,256,1024]{1,2,0:T(8,128)(2,1)}, u32[]{:S(2)}, u32[]{:S(2)}) async-start(bf16[4,256,1024]{1,2,0:T(8,128)(2,1)} %broadcast_in_dim.9), calls=%async_computation.4 | async-start | bytes 4194304 | tf_op jit(solution)/shard_map/all_to_all | solution.py:194
  136.1 109.2 %all-gather.12.cloned.1.call-start = ((), (), s32[]{:S(2)}) async-start(), calls=%async_computation.13 | async-start | bytes 2621440 | tf_op jit(solution)/shard_map/all_gather | solution.py:208
  165.7 82.9 %all-gather.8.cloned.1.call-start = ((), (), s32[]{:S(2)}) async-start(), calls=%async_computation.11 | async-start | bytes 2359296 | tf_op jit(solution)/shard_map/all_gather | solution.py:206
  211.9 33.3 %all-to-all-start.6 = ((bf16[8,288,128]{2,1,0:T(8,128)(2,1)}), bf16[8,288,128]{2,1,0:T(8,128)(2,1)}, u32[]{:S(2)}, u32[]{:S(2)}) async-start(bf16[8,288,128]{2,1,0:T(8,128)(2,1)} %pad_maximum_fusion.4), calls=%async_computation.6 | async-start | bytes 1179648 | tf_op jit(solution)/shard_map/all_to_all | solution.py:229
  216.1 82.5 %all-gather.10.cloned.1.call-start = ((), (), s32[]{:S(2)}) async-start(), calls=%async_computation.12 | async-start | bytes 2359296 | tf_op jit(solution)/shard_map/all_gather | solution.py:207
  216.7 7.5 %copy-start.9 = (bf16[256,1024]{1,0:T(8,128)(2,1)S(1)}, bf16[256,1024]{1,0:T(8,128)(2,1)}, u32[]{:S(2)}) copy-start(bf16[256,1024]{1,0:T(8,128)(2,1)} %convolution_convert_fusion.1) | copy-start | bytes 1572868
  251.7 47.0 %all-to-all-start.7 = ((bf16[4,256,1024]{2,1,0:T(8,128)(2,1)}), bf16[4,256,1024]{2,1,0:T(8,128)(2,1)}, u32[]{:S(2)}, u32[]{:S(2)}) async-start(bf16[4,256,1024]{2,1,0:T(8,128)(2,1)} %bitcast.126), calls=%async_computation.7 | async-start | bytes 4194304 | tf_op jit(solution)/shard_map/all_to_all | solution.py:233
  261.4 1.8 copy-start
  261.4 3.4 %copy-start.7 = (bf16[2048,512]{1,0:T(8,128)(2,1)S(1)}, bf16[2048,512]{1,0:T(8,128)(2,1)}, u32[]{:S(2)}) copy-start(bf16[2048,512]{1,0:T(8,128)(2,1)} %all-gather.12.cloned.1.call-done) | copy-start | bytes 6291460
  263.2 1.9 copy-start.2
  263.2 1.9 copy-start.4
  263.2 1.9 copy-start.6
  263.4 8.7 %collective-permute-start.1 = (bf16[6,3,1024]{2,0,1:T(8,128)(2,1)S(1)}, bf16[6,3,1024]{2,0,1:T(8,128)(2,1)S(1)}, u32[]{:S(2)}, u32[]{:S(2)}) collective-permute-start(bf16[6,3,1024]{2,0,1:T(8,128)(2,1)S(1)} %slice.146), channel_id=1, source_target_pairs={{4,0},{8,4},{12,8},{16,12},{20,16},{24,20},{28,24},{5,1},{9,5},{13... | collective-permute-start | bytes 110600 | tf_op jit(solution)/shard_map/ppermute | solution.py:12
  264.8 3.5 %copy-start.10 = (bf16[2048,512]{1,0:T(8,128)(2,1)S(1)}, bf16[2048,512]{1,0:T(8,128)(2,1)}, u32[]{:S(2)}) copy-start(bf16[2048,512]{1,0:T(8,128)(2,1)} %all-gather.8.cloned.1.call-done) | copy-start | bytes 6291460
  265.1 4.6 %copy-start.8 = (bf16[8,4,64,512]{3,2,1,0:T(8,128)(2,1)}, bf16[8,4,64,512]{3,2,1,0:T(8,128)(2,1)S(1)}, u32[]{:S(2)}) copy-start(bf16[8,4,64,512]{3,2,1,0:T(8,128)(2,1)S(1)} %copy.57) | copy-start | bytes 6291460
  268.4 3.7 %copy-start.1 = (bf16[256,1,1024]{2,0,1:T(8,128)(2,1)S(1)}, bf16[256,1,1024]{2,0,1:T(8,128)(2,1)}, u32[]{:S(2)}) copy-start(bf16[256,1,1024]{2,0,1:T(8,128)(2,1)} %fusion.15) | copy-start | bytes 1572868
  268.4 3.7 %copy-start.3 = (bf16[256,1,1024]{2,0,1:T(8,128)(2,1)S(1)}, bf16[256,1,1024]{2,0,1:T(8,128)(2,1)}, u32[]{:S(2)}) copy-start(bf16[256,1,1024]{2,0,1:T(8,128)(2,1)} %copy-done.2) | copy-start | bytes 1572868
  268.4 3.7 %copy-start.5 = (bf16[256,1,1024]{2,0,1:T(8,128)(2,1)S(1)}, bf16[256,1,1024]{2,0,1:T(8,128)(2,1)}, u32[]{:S(2)}) copy-start(bf16[256,1,1024]{2,0,1:T(8,128)(2,1)} %copy-done.4) | copy-start | bytes 1572868
  299.3 10.4 %all-to-all-start.8 = ((f32[8,21,128]{2,1,0:T(8,128)}), f32[8,21,128]{2,1,0:T(8,128)S(1)}, u32[]{:S(2)}, u32[]{:S(2)}) async-start(f32[8,21,128]{2,1,0:T(8,128)} %copy.58), calls=%async_computation.8 | async-start | bytes 196608 | tf_op jit(solution)/shard_map/all_to_all | solution.py:271
  310.4 10.4 %all-to-all-start.9 = ((f32[8,21,128]{2,1,0:T(8,128)}), f32[8,21,128]{2,1,0:T(8,128)S(1)}, u32[]{:S(2)}, u32[]{:S(2)}) async-start(f32[8,21,128]{2,1,0:T(8,128)} %broadcast_in_dim.11), calls=%async_computation.9 | async-start | bytes 196608 | tf_op jit(solution)/shard_map/all_to_all | solution.py:273
Sparse Core Ops, SparseCore 0:
  10.0 155.5 all-gather.5
  167.2 22.4 all-gather.11
  191.9 56.6 all-gather.7
  250.5 48.0 all-gather.9
